TPU v7x, 256 devices: a whole 4x4x8 slice. The times are simulated.
256 devices in a mesh: head: 4 (over z_hi), ctx: 64 (over x, y, z_lo, core).
Axes of the slice: x: 4, y: 4, z: 8 (z_hi: 4, z_lo: 2; z = z_hi * 2 + z_lo), core: 2. Of those that a mesh axis runs over, the one named last changes fastest.
Arguments:
- queries: bfloat16 [16384, 3584], P(('head', 'ctx')), may hold values from -6 to 6
- keys: bfloat16 [16384, 512], P(('head', 'ctx')), may hold values from -12 to 12
- values: bfloat16 [16384, 512], P(('head', 'ctx')), may hold values from -6 to 6
- block_index: int32 [128, 28, 128], replicated, may hold values from 0 to 127, as said below
- block_count: int32 [128, 28], replicated, may hold values from 1 to 128, as said below
- head_order: int32 [28], replicated, may hold values from 0 to 27, as said below
Outputs:
- attention_out: bfloat16 [16384, 3584], P(('head', 'ctx'))
Inputs may be any that keep to these rules, and one draw needn't show every extreme that they name: For query block b and head h the first block_count[b, h] entries of block_index[b, h] are distinct key blocks in ascending order, always including block 0 and block b and never above b; the later entries name the remaining blocks. block_count[b, h] is at most b + 1. `head_order`: A permutation of the 28 query heads; each aligned block of 7 entries that starts at a multiple of 7 holds heads of exactly two key and value heads (head // 7).
All inputs are finite; a program needn't handle non-finite values.
Results may differ from a plain program's by a relative error of at most 0.0045.
Values may be sent and summed in bfloat16 or wider, within the bound.
No kernel may reach another device: no remote copies, remote signals or barrier semaphores. Data moves between devices by JAX's collectives and lax.ppermute only.
A program may use at most 64 MiB of HBM per device.

v0:
```python
import math
from functools import partial

import jax
import jax.numpy as jnp
from jax import lax
from jax.experimental import pallas as pl
from jax.experimental.pallas import tpu as pltpu
from jax.sharding import Mesh, PartitionSpec as P

H = 28
KVH = 4
HD = 128
BLOCK = 128
GROUP = H // KVH
TILES = 4 * GROUP
NB = 8
FLOOR = -1e30
EXP_SCALE = math.log2(math.e) / math.sqrt(HD)
AXES = ("zhi", "x", "y", "zlo", "core")


def partner(array, axis, mask):
    return lax.ppermute(array, axis, [(i, i ^ mask) for i in range(lax.axis_size(axis))])


def swap_cores(array):
    return partner(array, "core", 1)


def tree(op, parts):
    while len(parts) > 1:
        parts = [op(*parts[i:i + 2]) if i + 1 < len(parts) else parts[i] for i in range(0, len(parts), 2)]
    return parts[0]


def attend_kernel(first, pieces, *refs):
    refs = list(refs)
    take = lambda n: [refs.pop(0) for _ in range(n)]
    tab, cnt = take(2)
    queries = take(2) if first else take(1)
    sources = take(pieces)
    state_in = [] if first else take(3)
    outs = take(4) if first else take(2)
    (kv,) = take(1)
    s_bufs, m_bufs, a_bufs = take(4), take(4), take(4)
    m_ref, l_ref, acc = outs[:3] if first else take(3)
    qt = outs[3] if first else queries[0]
    lse = None if first else take(1)[0]
    (sem,) = refs
    core = lax.axis_index("core")
    started, at = [], 0
    for source in sources:
        started.append(pltpu.make_async_copy(source, kv.at[pl.ds(at, source.shape[0])], sem))
        at += source.shape[0]
    for copy in started:
        copy.start()

    def chunks_of(t):
        return jnp.maximum((cnt[t] + (NB - 1)) // NB, 1)

    total = lax.fori_loop(0, TILES, lambda t, n: n + chunks_of(t), jnp.int32(0))
    keys = lax.broadcasted_iota(jnp.int32, (64, BLOCK), 0)
    rows = lax.broadcasted_iota(jnp.int32, (64, BLOCK), 1)
    seen = (keys <= rows) & (rows < 64) | (rows >= 64) & (core == 0)

    def start(t, _):
        if first:
            qt[t] = jnp.concatenate([queries[0][t], queries[1][t]], axis=0).T
            m_ref[t] = jnp.full((8, BLOCK), FLOOR, jnp.float32)
            l_ref[t] = jnp.zeros((8, BLOCK), jnp.float32)
            acc[t] = jnp.zeros((HD, BLOCK), jnp.float32)
        else:
            m_ref[t], l_ref[t], acc[t] = (ref[t] for ref in state_in)
        return 0

    lax.fori_loop(0, TILES, start, 0, unroll=2)
    m_ref[TILES] = jnp.zeros((8, BLOCK), jnp.float32)
    l_ref[TILES] = jnp.zeros((8, BLOCK), jnp.float32)
    acc[TILES] = jnp.zeros((HD, BLOCK), jnp.float32)
    for copy in started:
        copy.wait()

    def block(t, c, j, which):
        return kv[tab[t, c * NB + j], which]

    def products(t, c, s_ref, m_buf, a_buf):
        k = jnp.concatenate([block(t, c, j, 0) for j in range(NB)], axis=0)
        s = jnp.dot(k, qt[jnp.minimum(t, TILES - 1)], preferred_element_type=jnp.float32)
        left_over = cnt[t] - c * NB
        d = jnp.minimum(left_over, NB) - 1
        tops = []
        for j in range(NB):
            part = s[j * 64:(j + 1) * 64]
            top = jnp.max(part.reshape(8, 8, BLOCK), axis=0)
            tops.append(jnp.where((left_over > j) & ((d != j) | (left_over > NB)) if first else left_over > j, top, FLOOR))
            s_ref[j * 64:(j + 1) * 64] = jnp.where(left_over > j, part, FLOOR)
        if first:
            here = pl.ds(pl.multiple_of(d * 64, 64), 64)
            part = jnp.where(seen | (left_over > NB), s_ref[here, :], FLOOR)
            s_ref[here, :] = part
            tops.append(jnp.max(part.reshape(8, 8, BLOCK), axis=0))
        m_old = m_ref[t]
        m_new = jnp.maximum(m_old, jnp.max(tree(jnp.maximum, tops), axis=0, keepdims=True))
        m_ref[t] = m_new
        m_buf[...] = m_new
        a_buf[...] = jnp.exp2((m_old - m_new) * EXP_SCALE)

    def weigh(t, c, s_ref, m_buf, a_buf):
        m = m_buf[...][None]
        parts = []
        for j in range(NB):
            s = s_ref[j * 64:(j + 1) * 64].reshape(8, 8, BLOCK)
            parts.append(jnp.exp2((s - m) * EXP_SCALE).reshape(64, BLOCK))
        p = jnp.concatenate([part.astype(jnp.bfloat16) for part in parts], axis=0)
        part = tree(jnp.add, parts)
        part = tree(jnp.add, [part[i * 8:(i + 1) * 8] for i in range(8)])
        l_ref[t] = l_ref[t] * a_buf[...] + part
        v = jnp.concatenate([block(t, c, j, 1) for j in range(NB)], axis=0)
        update = lax.dot_general(
            v, p, (((0,), (0,)), ((), ())), preferred_element_type=jnp.float32
        )
        acc[t] = acc[t] * a_buf[:1] + update

    def steps(_, carry):
        items = list(carry)
        for k in range(8):
            t, c = items[0], items[1]
            old = (k - 3) % 8
            products(t, c, s_bufs[k % 4], m_bufs[k % 4], a_bufs[k % 4])
            weigh(items[6], items[7], s_bufs[old % 4], m_bufs[old % 4], a_bufs[old % 4])
            last = c + 1 >= chunks_of(t)
            items = [
                jnp.where(last, jnp.minimum(t + 1, TILES), t),
                jnp.where(last, 0, c + 1),
            ] + items[:6]
        return tuple(items)

    zero, dummy = jnp.int32(0), jnp.int32(TILES)
    lax.fori_loop(0, (total + 10) // 8, steps, (zero, zero) + (dummy, zero) * 3)
    if first:
        return
    o_own, o_oth = outs
    lse[...] = jnp.zeros_like(lse)

    def finish(t, _):
        whole = jnp.sum(l_ref[t], axis=0, keepdims=True)
        o = (acc[t] / whole).T.astype(jnp.bfloat16)
        o_own[t] = o[:64]
        o_oth[t] = o[64:]
        lse[pl.ds(t, 1), :] = m_ref[t][:1] * EXP_SCALE + jnp.log2(whole)
        return 0

    lax.fori_loop(0, TILES, finish, 0, unroll=2)
    rest = lse[...].T
    for i in range(3):
        part = rest.astype(jnp.bfloat16)
        o_own[TILES + i] = part[:64]
        o_oth[TILES + i] = part[64:]
        rest = rest - part.astype(jnp.float32)


def attend(tab, cnt, queries, pieces, state):
    vmem = pl.BlockSpec(memory_space=pltpu.VMEM)
    smem = pl.BlockSpec(memory_space=pltpu.SMEM)
    small = ((TILES + 1, 8, BLOCK), jnp.float32)
    large = ((TILES + 1, HD, BLOCK), jnp.float32)
    if state is None:
        shapes = [small, small, large, ((TILES, HD, BLOCK), jnp.bfloat16)]
        kept = []
    else:
        shapes = [((TILES + 3, 64, HD), jnp.bfloat16)] * 2
        kept = [pltpu.VMEM(*small), pltpu.VMEM(*small), pltpu.VMEM(*large)]
        kept += [pltpu.VMEM((BLOCK, BLOCK), jnp.float32)]
    slots = sum(piece.shape[0] for piece in pieces)
    flops = 2 * 2 * BLOCK * HD * 64 * TILES * slots // 2
    return pl.pallas_call(
        partial(attend_kernel, state is None, len(pieces)),
        out_shape=tuple(jax.ShapeDtypeStruct(*a) for a in shapes),
        in_specs=[smem, smem]
        + [vmem] * len(queries)
        + [pl.BlockSpec(memory_space=pl.ANY)] * len(pieces)
        + [vmem] * (0 if state is None else 3),
        out_specs=(vmem,) * len(shapes),
        scratch_shapes=[pltpu.VMEM((slots, 2, 64, HD), jnp.bfloat16)]
        + [pltpu.VMEM((NB * 64, BLOCK), jnp.float32)] * 4
        + [pltpu.VMEM((8, BLOCK), jnp.float32)] * 8
        + kept
        + [pltpu.SemaphoreType.DMA],
        compiler_params=pltpu.CompilerParams(vmem_limit_bytes=40 * 2**20),
        cost_estimate=pl.CostEstimate(
            flops=4 * flops, bytes_accessed=slots * 2**15, transcendentals=flops // 256
        ),
        name="attend",
    )(tab, cnt, *queries, *pieces, *(state or ()))


def merge_kernel(a, b, out):
    lse_a, lse_b = (
        sum(ref[TILES + i].astype(jnp.float32) for i in range(3)) for ref in (a, b)
    )
    top = jnp.maximum(lse_a, lse_b)
    w_a = jnp.exp2(lse_a - top)
    w_b = jnp.exp2(lse_b - top)
    w_a = w_a / (w_a + w_b)
    w_b = 1.0 - w_a
    for t in range(TILES):
        mixed = a[t].astype(jnp.float32) * w_a[:, t:t + 1]
        mixed = mixed + b[t].astype(jnp.float32) * w_b[:, t:t + 1]
        out[t] = mixed.astype(jnp.bfloat16)


def merge(a, b):
    vmem = pl.BlockSpec(memory_space=pltpu.VMEM)
    return pl.pallas_call(
        merge_kernel,
        out_shape=jax.ShapeDtypeStruct((TILES, 64, HD), jnp.bfloat16),
        in_specs=[vmem, vmem],
        out_specs=vmem,
        name="merge",
    )(a, b)


def place_kernel(order, heads, out):
    for j in range(H):
        out[:, j * HD:(j + 1) * HD] = heads[order[j]]


def place(order, heads):
    return pl.pallas_call(
        place_kernel,
        out_shape=jax.ShapeDtypeStruct((64, H * HD), jnp.bfloat16),
        in_specs=[
            pl.BlockSpec(memory_space=pltpu.SMEM),
            pl.BlockSpec(memory_space=pltpu.VMEM),
        ],
        out_specs=pl.BlockSpec(memory_space=pltpu.VMEM),
        name="place",
    )(order, heads)


def split_q_kernel(queries, out):
    for h in range(H):
        out[h] = queries[:, h * HD:(h + 1) * HD]


def split_kv_kernel(keys, values, out):
    for g in range(KVH):
        for copy in range(2):
            out[2 * g + copy, 0] = keys[:, g * HD:(g + 1) * HD]
            out[2 * g + copy, 1] = values[:, g * HD:(g + 1) * HD]


def split(kernel, shape, *arrays):
    vmem = pl.BlockSpec(memory_space=pltpu.VMEM)
    return pl.pallas_call(
        kernel,
        out_shape=jax.ShapeDtypeStruct(shape, jnp.bfloat16),
        in_specs=[vmem] * len(arrays),
        out_specs=vmem,
        name="split",
    )(*arrays)


def tables(block_index, block_count):
    here_x, here_y = lax.axis_index("x"), lax.axis_index("y")
    chip = (here_x * 4 + here_y) * 2 + lax.axis_index("zlo")
    group = lax.axis_index("zhi")
    index = block_index.reshape(4, 32, KVH, GROUP, 128)
    index = lax.dynamic_slice(index, (0, chip, group, 0, 0), (4, 1, 1, GROUP, 128))
    index = index.reshape(TILES, 128)
    count = block_count.reshape(4, 32, KVH, GROUP)
    count = lax.dynamic_slice(count, (0, chip, group, 0), (4, 1, 1, GROUP)).reshape(TILES, 1)

    z, inner = index // 32, index % 32
    rel_x, rel_y = (inner // 8) ^ here_x, (inner // 2 % 4) ^ here_y
    low = z < 2
    within, away = jnp.where(low, rel_x, rel_y), jnp.where(low, rel_y, rel_x)
    half = within // 2
    spot = jnp.where(half == 0, within, 3 - within) * 4 + z % 2 * 2 + inner % 2
    soon = away == jnp.where(half == 0, 1, 3)
    first = (away == 0) | soon
    slot_first = jnp.where(soon, 16, 0) + half * 8
    slot_second = half * 16 + jnp.where(away == 2, 8, 0)
    slot = jnp.where(first, slot_first, slot_second) + spot + jnp.where(low, 0, 32)
    entry = lax.broadcasted_iota(jnp.int32, (TILES, 128), 1)
    stage = jnp.where(entry < count, jnp.where(first, 0, 1), -1)
    before = lax.broadcasted_iota(jnp.int32, (128, 128), 0) <= lax.broadcasted_iota(
        jnp.int32, (128, 128), 1
    )
    result = []
    for number in range(2):
        member = stage == number
        rank = jnp.dot(
            member.astype(jnp.bfloat16), before.astype(jnp.bfloat16),
            preferred_element_type=jnp.float32,
        ).astype(jnp.int32)
        hit = (jnp.where(member, rank, 0)[:, :, None] - 1) == entry[:, None, :]
        packed = jnp.sum(jnp.where(hit, slot[:, :, None], 0), axis=1)
        packed = jnp.pad(packed, ((0, 1), (0, 0)))
        result.append((packed, jnp.pad(rank[:, 127], (0, 1), constant_values=1)))
    return result


def local(queries, keys, values, block_index, block_count, head_order):
    kv_sent = split(split_kv_kernel, (8, 2, 64, HD), keys, values)
    kv_got = lax.all_to_all(kv_sent, ("zhi", "zlo"), split_axis=0, concat_axis=0, tiled=True)
    low, high = kv_got[:4], kv_got[4:]
    low_next, high_next = partner(low, "x", 1), partner(high, "y", 1)
    q_sent = split(split_q_kernel, (H, 64, HD), queries)
    q_own = lax.all_to_all(
        q_sent.reshape(4, GROUP * 64, HD), "zhi", split_axis=0, concat_axis=0, tiled=True
    ).reshape(TILES, 64, HD)
    q_oth = swap_cores(q_own)
    early, late = [], []
    for mine, other, inner, outer in ((low, low_next, "x", "y"), (high, high_next, "y", "x")):
        one = jnp.concatenate([mine, other])
        two = partner(one, inner, 3)
        one_next, two_next = partner(one, outer, 1), partner(two, outer, 3)
        early += [one, two, one_next, two_next]
        late += [
            partner(jnp.concatenate([one, one_next]), outer, 3),
            partner(jnp.concatenate([two, two_next]), outer, 1),
        ]
    ready, arriving = tables(block_index, block_count)
    *state, turned = attend(*ready, [q_own, q_oth], early, None)
    mine, others = attend(*arriving, [turned], late, state)
    attended = merge(mine, swap_cores(others))
    returned = lax.all_to_all(
        attended.reshape(4, GROUP * 64, HD), "zhi", split_axis=0, concat_axis=0, tiled=True
    ).reshape(H, 64, HD)
    return place(head_order, returned)


def solution(mesh):
    wide = Mesh(mesh.devices.reshape(4, 4, 4, 2, 2), AXES)
    tokens = P(AXES, None)
    return jax.shard_map(
        local,
        mesh=wide,
        in_specs=(tokens, tokens, tokens, P(), P(), P()),
        out_specs=tokens,
        check_vma=False,
    )
```

profile of v0, /device:TPU:46, one launch (start us, length us, event | category | flops | bytes accessed | tf_op | source)
XLA Modules:
  0.0 111.9 jit_solution(8708038456285312133)
XLA Ops:
  0.0 1.7 %split.3 = bf16[8,2,64,128]{3,2,1,0:T(8,128)(2,1)} custom-call(bf16[64,512]{1,0:T(8,128)(2,1)} %keys.1, bf16[64,512]{1,0:T(8,128)(2,1)} %values.1), custom_call_target="tpu_custom_call" | custom-call | tf_op jit(solution)/shard_map/split/pallas_call | solution.py:256
  1.8 8.6 %all-to-all-start.1 = ((bf16[8,2,64,128]{3,2,1,0:T(8,128)(2,1)}), bf16[8,2,64,128]{3,2,1,0:T(8,128)(2,1)S(1)}, u32[]{:S(2)}, u32[]{:S(2)}) async-start(bf16[8,2,64,128]{3,2,1,0:T(8,128)(2,1)} %split.3), calls=%async_computation.1 | async-start | bytes 524288 | tf_op jit(solution)/shard_map/all_to_all | solution.py:307
  11.5 1.9 %split.2 = bf16[28,64,128]{2,1,0:T(8,128)(2,1)} custom-call(bf16[64,3584]{1,0:T(8,128)(2,1)} %queries.1), custom_call_target="tpu_custom_call" | custom-call | tf_op jit(solution)/shard_map/split/pallas_call | solution.py:256
  13.6 7.1 %all-to-all-done.1 = bf16[8,2,64,128]{3,2,1,0:T(8,128)(2,1)S(1)} async-done(((bf16[8,2,64,128]{3,2,1,0:T(8,128)(2,1)}), bf16[8,2,64,128]{3,2,1,0:T(8,128)(2,1)S(1)}, u32[]{:S(2)}, u32[]{:S(2)}) %all-to-all-start.1) | async-done | bytes 262176 | tf_op jit(solution)/shard_map/all_to_all | solution.py:307
  20.7 3.5 %all-to-all-start = ((bf16[4,448,128]{2,1,0:T(8,128)(2,1)}), bf16[4,448,128]{2,1,0:T(8,128)(2,1)S(1)}, u32[]{:S(2)}, u32[]{:S(2)}) async-start(bf16[4,448,128]{2,1,0:T(8,128)(2,1)} %bitcast.14), calls=%async_computation | async-start | bytes 917504 | tf_op jit(solution)/shard_map/all_to_all | solution.py:311
  25.8 3.5 %collective-permute-done.1 = bf16[4,2,64,128]{3,2,1,0:T(8,128)(2,1)S(1)} collective-permute-done((bf16[4,2,64,128]{3,2,1,0:T(8,128)(2,1)S(1)}, bf16[4,2,64,128]{3,2,1,0:T(8,128)(2,1)S(1)}, u32[]{:S(2)}, u32[]{:S(2)}) %collective-permute-start.1) | collective-permute-done | bytes 131104 | tf_op jit(solution)/shard_map/ppermute | solution.py:24
  31.3 2.2 %collective-permute-start.6 = (bf16[8,2,64,128]{3,2,1,0:T(8,128)(2,1)S(1)}, bf16[8,2,64,128]{3,2,1,0:T(8,128)(2,1)}, u32[]{:S(2)}, u32[]{:S(2)}) collective-permute-start(bf16[8,2,64,128]{3,2,1,0:T(8,128)(2,1)S(1)} %pad_maximum_fusion.5.refs_8_), channel_id=1, source_target_pairs={{0,12},{4,8},{8,4},{12,0},{1,13},{5,9},{9,5},{13,1},{2,14},{6,10},... | collective-permute-start | bytes 786440 | tf_op jit(solution)/shard_map/ppermute | solution.py:24
  33.5 2.2 %select_reduce_fusion = (s32[28,128]{1,0:T(8,128)S(1)}, s32[28,128]{1,0:T(8,128)S(1)}) fusion(s32[28,128]{1,0:T(8,128)S(1)} %get-tuple-element.24, s32[28,128]{1,0:T(8,128)S(1)} %get-tuple-element.19, s32[28,128]{1,0:T(8,128)S(1)} %get-tuple-element.23), kind=kLoop, calls=%fused_computation | loop fusion | flops 2745344 | bytes 71680 | tf_op jit(solution)/shard_map/reduce_sum | solution.py:299
  35.7 1.0 collective-permute-start.7
  37.7 1.6 %collective-permute-start.4 = (bf16[8,2,64,128]{3,2,1,0:T(8,128)(2,1)S(1)}, bf16[8,2,64,128]{3,2,1,0:T(8,128)(2,1)}, u32[]{:S(2)}, u32[]{:S(2)}) collective-permute-start(bf16[8,2,64,128]{3,2,1,0:T(8,128)(2,1)S(1)} %collective-permute-done.2.refs_5_), channel_id=1, source_target_pairs={{0,12},{4,8},{8,4},{12,0},{1,13},{5,9},{9,5},{13,1},{2,14},{6,10},... | collective-permute-start | bytes 786440 | tf_op jit(solution)/shard_map/ppermute | solution.py:24
  40.5 2.0 %collective-permute-start.8 = (bf16[8,2,64,128]{3,2,1,0:T(8,128)(2,1)}, bf16[8,2,64,128]{3,2,1,0:T(8,128)(2,1)S(1)}, u32[]{:S(2)}, u32[]{:S(2)}) collective-permute-start(bf16[8,2,64,128]{3,2,1,0:T(8,128)(2,1)} %collective-permute-done.6.refs_9_), channel_id=1, source_target_pairs={{0,48},{16,32},{32,16},{48,0},{1,49},{17,33},{33,17},{49,1},{2,50}... | collective-permute-start | bytes 786440 | tf_op jit(solution)/shard_map/ppermute | solution.py:24
  42.4 1.0 pad_maximum_fusion
  43.4 1.0 collective-permute-start.9
  44.4 1.0 pad_maximum_fusion.2
  45.4 2.8 %collective-permute-start.11 = (bf16[16,2,64,128]{3,2,1,0:T(8,128)(2,1)S(1)}, bf16[16,2,64,128]{3,2,1,0:T(8,128)(2,1)S(1)}, u32[]{:S(2)}, u32[]{:S(2)}) collective-permute-start(bf16[16,2,64,128]{3,2,1,0:T(8,128)(2,1)S(1)} %pad_maximum_fusion.2), channel_id=1, source_target_pairs={{0,48},{16,32},{32,16},{48,0},{1,49},{17,33},{33,17},{49,1},{2,50}... | collective-permute-start | bytes 1572872 | tf_op jit(solution)/shard_map/ppermute | solution.py:24
  48.3 1.0 pad_maximum_fusion.1
  49.3 2.2 %collective-permute-start.10 = (bf16[16,2,64,128]{3,2,1,0:T(8,128)(2,1)S(1)}, bf16[16,2,64,128]{3,2,1,0:T(8,128)(2,1)S(1)}, u32[]{:S(2)}, u32[]{:S(2)}) collective-permute-start(bf16[16,2,64,128]{3,2,1,0:T(8,128)(2,1)S(1)} %pad_maximum_fusion.1), channel_id=1, source_target_pairs={{0,4},{4,0},{8,12},{12,8},{1,5},{5,1},{9,13},{13,9},{2,6},{6,2},{1... | collective-permute-start | bytes 1572872 | tf_op jit(solution)/shard_map/ppermute | solution.py:24
  51.5 1.0 pad_maximum_fusion.3
  52.6 13.8 %attend.2 = (f32[29,8,128]{2,1,0:T(8,128)S(1)}, f32[29,8,128]{2,1,0:T(8,128)S(1)}, f32[29,128,128]{2,1,0:T(8,128)S(1)}, bf16[28,128,128]{2,1,0:T(8,128)(2,1)S(1)}) custom-call(s32[29,128]{1,0:T(8,128)S(1)} %pad.16.refs_0_, s32[29]{0:T(128)S(1)} %pad.17.refs_1_, bf16[28,64,128]{2,1,0:T(8,128)(2,1)S(1)} %bitcast.13, ...), custom_call_target="tpu_custom_call" | custom-call | flops 15032385536 | bytes 2097152 | tf_op jit(solution)/shard_map/attend/pallas_call | solution.py:177
  66.5 15.7 %attend.3 = (bf16[31,64,128]{2,1,0:T(8,128)(2,1)S(1)}, bf16[31,64,128]{2,1,0:T(8,128)(2,1)S(1)}) custom-call(s32[29,128]{1,0:T(8,128)S(1)} %pad.14.refs_0_, s32[29]{0:T(128)S(1)} %pad.15.refs_1_, bf16[28,128,128]{2,1,0:T(8,128)(2,1)S(1)} %get-tuple-element.11.refs_2_, bf16[16,2,64,128]{3,2,1,0:T(8,128)(2,1)S(1)} %collective-permute-done.9.refs_3_, ...), custom_call_target="tpu_custom_call" | custom-call | flops 15032385536 | bytes 2097152 | tf_op jit(solution)/shard_map/attend/pallas_call | solution.py:177
  83.0 1.9 %collective-permute-done.13.b = bf16[31,64,128]{2,1,0:T(8,128)(2,1)S(1)} collective-permute-done((bf16[31,64,128]{2,1,0:T(8,128)(2,1)S(1)}, bf16[31,64,128]{2,1,0:T(8,128)(2,1)S(1)}, u32[]{:S(2)}, u32[]{:S(2)}) %collective-permute-start.13) | collective-permute-done | bytes 507936 | tf_op jit(solution)/shard_map/ppermute | solution.py:24
  85.7 2.6 %merge.1 = bf16[28,64,128]{2,1,0:T(8,128)(2,1)} custom-call(bf16[31,64,128]{2,1,0:T(8,128)(2,1)} %copy-done.1, bf16[31,64,128]{2,1,0:T(8,128)(2,1)} %copy-done.5), custom_call_target="tpu_custom_call" | custom-call | tf_op jit(solution)/shard_map/merge/pallas_call | solution.py:215
  88.2 21.7 %all_to_all.15 = bf16[4,448,128]{2,1,0:T(8,128)(2,1)} all-to-all(bf16[4,448,128]{2,1,0:T(8,128)(2,1)} %bitcast.16), channel_id=1, replica_groups=mesh['zhi'=4,'x'=4,'y'=4,'zlo'=2,'core'=2] {'zhi'}, dimensions={0} | all-to-all | bytes 917504 | tf_op jit(solution)/shard_map/all_to_all | solution.py:329
  110.0 1.9 %place.1 = bf16[64,3584]{1,0:T(8,128)(2,1)} custom-call(s32[28]{0:T(128)} %order.1, bf16[28,64,128]{2,1,0:T(8,128)(2,1)} %bitcast.15), custom_call_target="tpu_custom_call" | custom-call | tf_op jit(solution)/shard_map/place/pallas_call | solution.py:230
  (51 shorter events, 8.8 us)
Async XLA Ops:
  0.0 11.1 %copy-start = (s32[128,28,128]{2,0,1:T(8,128)S(1)}, s32[128,28,128]{2,0,1:T(8,128)}, u32[]{:S(2)}) copy-start(s32[128,28,128]{2,0,1:T(8,128)} %param.9) | copy-start | bytes 5505028
  1.8 19.0 %all-to-all-start.1 = ((bf16[8,2,64,128]{3,2,1,0:T(8,128)(2,1)}), bf16[8,2,64,128]{3,2,1,0:T(8,128)(2,1)S(1)}, u32[]{:S(2)}, u32[]{:S(2)}) async-start(bf16[8,2,64,128]{3,2,1,0:T(8,128)(2,1)} %split.3), calls=%async_computation.1 | async-start | bytes 524288 | tf_op jit(solution)/shard_map/all_to_all | solution.py:307
  20.7 18.7 %all-to-all-start = ((bf16[4,448,128]{2,1,0:T(8,128)(2,1)}), bf16[4,448,128]{2,1,0:T(8,128)(2,1)S(1)}, u32[]{:S(2)}, u32[]{:S(2)}) async-start(bf16[4,448,128]{2,1,0:T(8,128)(2,1)} %bitcast.14), calls=%async_computation | async-start | bytes 917504 | tf_op jit(solution)/shard_map/all_to_all | solution.py:311
  24.2 5.1 %copy-start.2 = (bf16[4,2,64,128]{3,2,1,0:T(8,128)(2,1)}, bf16[4,2,64,128]{3,2,1,0:T(8,128)(2,1)S(1)}, u32[]{:S(2)}) copy-start(bf16[4,2,64,128]{3,2,1,0:T(8,128)(2,1)S(1)} %get-tuple-element.22) | copy-start | bytes 393220
  24.3 5.1 %collective-permute-start.1 = (bf16[4,2,64,128]{3,2,1,0:T(8,128)(2,1)S(1)}, bf16[4,2,64,128]{3,2,1,0:T(8,128)(2,1)S(1)}, u32[]{:S(2)}, u32[]{:S(2)}) collective-permute-start(bf16[4,2,64,128]{3,2,1,0:T(8,128)(2,1)S(1)} %get-tuple-element.22), channel_id=1, source_target_pairs={{0,16},{16,0},{32,48},{48,32},{1,17},{17,1},{33,49},{49,33},{2,18}... | collective-permute-start | bytes 393224 | tf_op jit(solution)/shard_map/ppermute | solution.py:24
  25.2 6.1 %collective-permute-start.5 = (bf16[4,2,64,128]{3,2,1,0:T(8,128)(2,1)S(1)}, bf16[4,2,64,128]{3,2,1,0:T(8,128)(2,1)S(1)}, u32[]{:S(2)}, u32[]{:S(2)}) collective-permute-start(bf16[4,2,64,128]{3,2,1,0:T(8,128)(2,1)S(1)} %get-tuple-element.21), channel_id=1, source_target_pairs={{0,4},{4,0},{8,12},{12,8},{1,5},{5,1},{9,13},{13,9},{2,6},{6,2},{1... | collective-permute-start | bytes 393224 | tf_op jit(solution)/shard_map/ppermute | solution.py:24
  29.3 0.7 copy-start.4
  30.0 7.7 %collective-permute-start.2 = (bf16[8,2,64,128]{3,2,1,0:T(8,128)(2,1)S(1)}, bf16[8,2,64,128]{3,2,1,0:T(8,128)(2,1)S(1)}, u32[]{:S(2)}, u32[]{:S(2)}) collective-permute-start(bf16[8,2,64,128]{3,2,1,0:T(8,128)(2,1)S(1)} %pad_maximum_fusion.4.refs_4_), channel_id=1, source_target_pairs={{0,48},{16,32},{32,16},{48,0},{1,49},{17,33},{33,17},{49,1},{2,50}... | collective-permute-start | bytes 786440 | tf_op jit(solution)/shard_map/ppermute | solution.py:24
  30.6 11.9 %collective-permute-start.3 = (bf16[8,2,64,128]{3,2,1,0:T(8,128)(2,1)S(1)}, bf16[8,2,64,128]{3,2,1,0:T(8,128)(2,1)S(1)}, u32[]{:S(2)}, u32[]{:S(2)}) collective-permute-start(bf16[8,2,64,128]{3,2,1,0:T(8,128)(2,1)S(1)} %pad_maximum_fusion.4.refs_4_), channel_id=1, source_target_pairs={{0,4},{4,0},{8,12},{12,8},{1,5},{5,1},{9,13},{13,9},{2,6},{6,2},{1... | collective-permute-start | bytes 786440 | tf_op jit(solution)/shard_map/ppermute | solution.py:24
  31.3 8.2 %copy-start.3 = (bf16[4,2,64,128]{3,2,1,0:T(8,128)(2,1)}, bf16[4,2,64,128]{3,2,1,0:T(8,128)(2,1)S(1)}, u32[]{:S(2)}) copy-start(bf16[4,2,64,128]{3,2,1,0:T(8,128)(2,1)S(1)} %collective-permute-done.5) | copy-start | bytes 393220
  31.3 9.1 %collective-permute-start.6 = (bf16[8,2,64,128]{3,2,1,0:T(8,128)(2,1)S(1)}, bf16[8,2,64,128]{3,2,1,0:T(8,128)(2,1)}, u32[]{:S(2)}, u32[]{:S(2)}) collective-permute-start(bf16[8,2,64,128]{3,2,1,0:T(8,128)(2,1)S(1)} %pad_maximum_fusion.5.refs_8_), channel_id=1, source_target_pairs={{0,12},{4,8},{8,4},{12,0},{1,13},{5,9},{9,5},{13,1},{2,14},{6,10},... | collective-permute-start | bytes 786440 | tf_op jit(solution)/shard_map/ppermute | solution.py:24
  35.7 8.7 %collective-permute-start.7 = (bf16[8,2,64,128]{3,2,1,0:T(8,128)(2,1)S(1)}, bf16[8,2,64,128]{3,2,1,0:T(8,128)(2,1)}, u32[]{:S(2)}, u32[]{:S(2)}) collective-permute-start(bf16[8,2,64,128]{3,2,1,0:T(8,128)(2,1)S(1)} %pad_maximum_fusion.5.refs_8_), channel_id=1, source_target_pairs={{0,16},{16,0},{32,48},{48,32},{1,17},{17,1},{33,49},{49,33},{2,18}... | collective-permute-start | bytes 786440 | tf_op jit(solution)/shard_map/ppermute | solution.py:24
  37.7 10.6 %collective-permute-start.4 = (bf16[8,2,64,128]{3,2,1,0:T(8,128)(2,1)S(1)}, bf16[8,2,64,128]{3,2,1,0:T(8,128)(2,1)}, u32[]{:S(2)}, u32[]{:S(2)}) collective-permute-start(bf16[8,2,64,128]{3,2,1,0:T(8,128)(2,1)S(1)} %collective-permute-done.2.refs_5_), channel_id=1, source_target_pairs={{0,12},{4,8},{8,4},{12,0},{1,13},{5,9},{9,5},{13,1},{2,14},{6,10},... | collective-permute-start | bytes 786440 | tf_op jit(solution)/shard_map/ppermute | solution.py:24
  39.5 13.1 %collective-permute-start = (bf16[28,64,128]{2,1,0:T(8,128)(2,1)S(1)}, bf16[28,64,128]{2,1,0:T(8,128)(2,1)S(1)}, u32[]{:S(2)}, u32[]{:S(2)}) collective-permute-start(bf16[28,64,128]{2,1,0:T(8,128)(2,1)S(1)} %bitcast.12), channel_id=1, source_target_pairs={{0,1},{1,0},{2,3},{3,2},{4,5},{5,4},{6,7},{7,6},{8,9},{9,8},{10,11... | collective-permute-start | bytes 1376264 | tf_op jit(solution)/shard_map/ppermute | solution.py:24
  40.5 11.0 %collective-permute-start.8 = (bf16[8,2,64,128]{3,2,1,0:T(8,128)(2,1)}, bf16[8,2,64,128]{3,2,1,0:T(8,128)(2,1)S(1)}, u32[]{:S(2)}, u32[]{:S(2)}) collective-permute-start(bf16[8,2,64,128]{3,2,1,0:T(8,128)(2,1)} %collective-permute-done.6.refs_9_), channel_id=1, source_target_pairs={{0,48},{16,32},{32,16},{48,0},{1,49},{17,33},{33,17},{49,1},{2,50}... | collective-permute-start | bytes 786440 | tf_op jit(solution)/shard_map/ppermute | solution.py:24
  43.4 23.0 %collective-permute-start.9 = (bf16[16,2,64,128]{3,2,1,0:T(8,128)(2,1)S(1)}, bf16[16,2,64,128]{3,2,1,0:T(8,128)(2,1)S(1)}, u32[]{:S(2)}, u32[]{:S(2)}) collective-permute-start(bf16[16,2,64,128]{3,2,1,0:T(8,128)(2,1)S(1)} %pad_maximum_fusion), channel_id=1, source_target_pairs={{0,12},{4,8},{8,4},{12,0},{1,13},{5,9},{9,5},{13,1},{2,14},{6,10},... | collective-permute-start | bytes 1572872 | tf_op jit(solution)/shard_map/ppermute | solution.py:24
  45.4 21.0 %collective-permute-start.11 = (bf16[16,2,64,128]{3,2,1,0:T(8,128)(2,1)S(1)}, bf16[16,2,64,128]{3,2,1,0:T(8,128)(2,1)S(1)}, u32[]{:S(2)}, u32[]{:S(2)}) collective-permute-start(bf16[16,2,64,128]{3,2,1,0:T(8,128)(2,1)S(1)} %pad_maximum_fusion.2), channel_id=1, source_target_pairs={{0,48},{16,32},{32,16},{48,0},{1,49},{17,33},{33,17},{49,1},{2,50}... | collective-permute-start | bytes 1572872 | tf_op jit(solution)/shard_map/ppermute | solution.py:24
  49.3 17.2 %collective-permute-start.10 = (bf16[16,2,64,128]{3,2,1,0:T(8,128)(2,1)S(1)}, bf16[16,2,64,128]{3,2,1,0:T(8,128)(2,1)S(1)}, u32[]{:S(2)}, u32[]{:S(2)}) collective-permute-start(bf16[16,2,64,128]{3,2,1,0:T(8,128)(2,1)S(1)} %pad_maximum_fusion.1), channel_id=1, source_target_pairs={{0,4},{4,0},{8,12},{12,8},{1,5},{5,1},{9,13},{13,9},{2,6},{6,2},{1... | collective-permute-start | bytes 1572872 | tf_op jit(solution)/shard_map/ppermute | solution.py:24
  52.5 14.0 %collective-permute-start.12 = (bf16[16,2,64,128]{3,2,1,0:T(8,128)(2,1)S(1)}, bf16[16,2,64,128]{3,2,1,0:T(8,128)(2,1)S(1)}, u32[]{:S(2)}, u32[]{:S(2)}) collective-permute-start(bf16[16,2,64,128]{3,2,1,0:T(8,128)(2,1)S(1)} %pad_maximum_fusion.3), channel_id=1, source_target_pairs={{0,16},{16,0},{32,48},{48,32},{1,17},{17,1},{33,49},{49,33},{2,18}... | collective-permute-start | bytes 1572872 | tf_op jit(solution)/shard_map/ppermute | solution.py:24
  82.2 0.8 copy-start.1
  83.0 1.9 %collective-permute-start.13 = (bf16[31,64,128]{2,1,0:T(8,128)(2,1)S(1)}, bf16[31,64,128]{2,1,0:T(8,128)(2,1)S(1)}, u32[]{:S(2)}, u32[]{:S(2)}) collective-permute-start(bf16[31,64,128]{2,1,0:T(8,128)(2,1)S(1)} %get-tuple-element.16), channel_id=1, source_target_pairs={{0,1},{1,0},{2,3},{3,2},{4,5},{5,4},{6,7},{7,6},{8,9},{9,8},{10,11... | collective-permute-start | bytes 1523720 | tf_op jit(solution)/shard_map/ppermute | solution.py:24
  84.9 0.8 copy-start.5
where the time goes:
time: 114 us; the launch traced here: 112 us
  Pallas kernels  37.6 us (33%)
  starting transfers between devices  27.3 us (24%)
  blocking collectives  21.7 us (19%)
  waiting for transfers between devices  14.5 us (13%)
  other arithmetic  6.34 us (6%)
  local copies, waits for them, and re-layouts  3.75 us (3%)
    pallas_call x2, Pallas kernels, attend(): pl.pallas_call(partial(attend_kernel, state is None, len(pieces)), out_sh...  29.5 us
    all_to_all x1, blocking collectives, local(): lax.all_to_all(attended.reshape(4, GROUP * 64, HD), 'zhi', split_axis=0,...  21.7 us
    ppermute x14, starting transfers between devices, partner(): lax.ppermute(array, axis, [(i, i ^ mask) for i in range(lax.axis_size(axi...  15.3 us
    all_to_all x1, starting transfers between devices, local(): lax.all_to_all(kv_sent, ('zhi', 'zlo'), split_axis=0, concat_axis=0, tile...  8.57 us
    ppermute x14, waiting for transfers between devices, partner(): lax.ppermute(array, axis, [(i, i ^ mask) for i in range(lax.axis_size(axi...  7.37 us
    all_to_all x1, waiting for transfers between devices, local(): lax.all_to_all(kv_sent, ('zhi', 'zlo'), split_axis=0, concat_axis=0, tile...  7.13 us
    pallas_call x2, Pallas kernels, split(): pl.pallas_call(kernel, out_shape=jax.ShapeDtypeStruct(shape, jnp.bfloat16...  3.61 us
    all_to_all x1, starting transfers between devices, local(): lax.all_to_all(q_sent.reshape(4, GROUP * 64, HD), 'zhi', split_axis=0, co...  3.47 us
  transfers between devices with their start and end apart: 16, of which 6 were waited for; matrix products, arithmetic and copies ran while one was open for 7% of the time, Pallas kernels for 14%

commit v1 on v0

--- a/solution.py
+++ b/solution.py
@@ -46,7 +46,7 @@
     s_bufs, m_bufs, a_bufs = take(4), take(4), take(4)
     m_ref, l_ref, acc = outs[:3] if first else take(3)
     qt = outs[3] if first else queries[0]
-    lse = None if first else take(1)[0]
+    lse, whole_out = (None, None) if first else take(2)
     (sem,) = refs
     core = lax.axis_index("core")
     started, at = [], 0
@@ -140,24 +140,34 @@
     lax.fori_loop(0, (total + 10) // 8, steps, (zero, zero) + (dummy, zero) * 3)
     if first:
         return
-    o_own, o_oth = outs
     lse[...] = jnp.zeros_like(lse)
 
     def finish(t, _):
         whole = jnp.sum(l_ref[t], axis=0, keepdims=True)
-        o = (acc[t] / whole).T.astype(jnp.bfloat16)
-        o_own[t] = o[:64]
-        o_oth[t] = o[64:]
+        whole_out[t] = (acc[t] / whole).T
         lse[pl.ds(t, 1), :] = m_ref[t][:1] * EXP_SCALE + jnp.log2(whole)
         return 0
 
-    lax.fori_loop(0, TILES, finish, 0, unroll=2)
-    rest = lse[...].T
-    for i in range(3):
-        part = rest.astype(jnp.bfloat16)
-        o_own[TILES + i] = part[:64]
-        o_oth[TILES + i] = part[64:]
-        rest = rest - part.astype(jnp.float32)
+    leaving = []
+
+    def leave(at, count):
+        for i, out in enumerate(outs):
+            leaving.append(
+                pltpu.make_async_copy(
+                    whole_out.at[pl.ds(at, count), pl.ds(i * 64, 64)],
+                    out.at[pl.ds(at, count)],
+                    sem,
+                )
+            )
+            leaving[-1].start()
+
+    for stripe in range(4):
+        lax.fori_loop(stripe * GROUP, (stripe + 1) * GROUP, finish, 0, unroll=GROUP)
+        leave(stripe * GROUP, GROUP)
+    whole_out[TILES] = lse[...].T
+    leave(TILES, 1)
+    for copy in leaving:
+        copy.wait()
 
 
 def attend(tab, cnt, queries, pieces, state):
@@ -169,9 +179,9 @@
         shapes = [small, small, large, ((TILES, HD, BLOCK), jnp.bfloat16)]
         kept = []
     else:
-        shapes = [((TILES + 3, 64, HD), jnp.bfloat16)] * 2
+        shapes = [((TILES + 1, 64, HD), jnp.float32)] * 2
         kept = [pltpu.VMEM(*small), pltpu.VMEM(*small), pltpu.VMEM(*large)]
-        kept += [pltpu.VMEM((BLOCK, BLOCK), jnp.float32)]
+        kept += [pltpu.VMEM((BLOCK, BLOCK), jnp.float32), pltpu.VMEM(*large)]
     slots = sum(piece.shape[0] for piece in pieces)
     flops = 2 * 2 * BLOCK * HD * 64 * TILES * slots // 2
     return pl.pallas_call(
@@ -181,7 +191,7 @@
         + [vmem] * len(queries)
         + [pl.BlockSpec(memory_space=pl.ANY)] * len(pieces)
         + [vmem] * (0 if state is None else 3),
-        out_specs=(vmem,) * len(shapes),
+        out_specs=(vmem if state is None else pl.BlockSpec(memory_space=pltpu.HBM),) * len(shapes),
         scratch_shapes=[pltpu.VMEM((slots, 2, 64, HD), jnp.bfloat16)]
         + [pltpu.VMEM((NB * 64, BLOCK), jnp.float32)] * 4
         + [pltpu.VMEM((8, BLOCK), jnp.float32)] * 8
@@ -195,38 +205,67 @@
     )(tab, cnt, *queries, *pieces, *(state or ()))
 
 
-def merge_kernel(a, b, out):
-    lse_a, lse_b = (
-        sum(ref[TILES + i].astype(jnp.float32) for i in range(3)) for ref in (a, b)
-    )
-    top = jnp.maximum(lse_a, lse_b)
-    w_a = jnp.exp2(lse_a - top)
-    w_b = jnp.exp2(lse_b - top)
-    w_a = w_a / (w_a + w_b)
-    w_b = 1.0 - w_a
-    for t in range(TILES):
-        mixed = a[t].astype(jnp.float32) * w_a[:, t:t + 1]
-        mixed = mixed + b[t].astype(jnp.float32) * w_b[:, t:t + 1]
-        out[t] = mixed.astype(jnp.bfloat16)
+def merge_kernel(a_far, b_far, out_far, a, b, out, sems):
+    spans = [(TILES, 1)] + [(i * GROUP, GROUP) for i in range(4)]
+    arriving = [
+        [
+            pltpu.make_async_copy(
+                far.at[pl.ds(at, count)], near.at[pl.ds(at, count)], sems.at[2 * i + k]
+            )
+            for k, (far, near) in enumerate(((a_far, a), (b_far, b)))
+        ]
+        for i, (at, count) in enumerate(spans)
+    ]
+    for copies in arriving:
+        for copy in copies:
+            copy.start()
+    leaving = []
+    for i, (at, count) in enumerate(spans):
+        for copy in arriving[i]:
+            copy.wait()
+        if i == 0:
+            top = jnp.maximum(a[TILES], b[TILES])
+            w_a = jnp.exp2(a[TILES] - top)
+            w_b = jnp.exp2(b[TILES] - top)
+            w_a = w_a / (w_a + w_b)
+            w_b = 1.0 - w_a
+            continue
+        for t in range(at, at + count):
+            out[t] = (a[t] * w_a[:, t:t + 1] + b[t] * w_b[:, t:t + 1]).astype(jnp.bfloat16)
+        leaving.append(
+            pltpu.make_async_copy(
+                out.at[pl.ds(at, count)], out_far.at[pl.ds(at, count)], sems.at[9 + i]
+            )
+        )
+        leaving[-1].start()
+    for copy in leaving:
+        copy.wait()
 
 
 def merge(a, b):
-    vmem = pl.BlockSpec(memory_space=pltpu.VMEM)
+    far = pl.BlockSpec(memory_space=pltpu.HBM)
+    part = pltpu.VMEM((TILES + 1, 64, HD), jnp.float32)
     return pl.pallas_call(
         merge_kernel,
         out_shape=jax.ShapeDtypeStruct((TILES, 64, HD), jnp.bfloat16),
-        in_specs=[vmem, vmem],
-        out_specs=vmem,
+        in_specs=[far, far],
+        out_specs=far,
+        scratch_shapes=[
+            part, part, pltpu.VMEM((TILES, 64, HD), jnp.bfloat16), pltpu.SemaphoreType.DMA((14,))
+        ],
         name="merge",
     )(a, b)
 
 
-def place_kernel(order, heads, out):
-    for j in range(H):
-        out[:, j * HD:(j + 1) * HD] = heads[order[j]]
+def place_kernel(spot, heads, out):
+    for h in range(H):
+        at = pl.multiple_of(spot[h] * HD, HD)
+        out[:, pl.ds(at, HD)] = heads[h]
 
 
 def place(order, heads):
+    heads_iota = jnp.arange(H, dtype=jnp.int32)
+    spot = jnp.sum(jnp.where(order[:, None] == heads_iota[None], heads_iota[:, None], 0), axis=0)
     return pl.pallas_call(
         place_kernel,
         out_shape=jax.ShapeDtypeStruct((64, H * HD), jnp.bfloat16),
@@ -236,7 +275,7 @@
         ],
         out_specs=pl.BlockSpec(memory_space=pltpu.VMEM),
         name="place",
-    )(order, heads)
+    )(spot, heads)
 
 
 def split_q_kernel(queries, out):
@@ -251,13 +290,13 @@
             out[2 * g + copy, 1] = values[:, g * HD:(g + 1) * HD]
 
 
-def split(kernel, shape, *arrays):
+def split(kernel, shapes, *arrays):
     vmem = pl.BlockSpec(memory_space=pltpu.VMEM)
     return pl.pallas_call(
         kernel,
-        out_shape=jax.ShapeDtypeStruct(shape, jnp.bfloat16),
+        out_shape=tuple(jax.ShapeDtypeStruct(shape, jnp.bfloat16) for shape in shapes),
         in_specs=[vmem] * len(arrays),
-        out_specs=vmem,
+        out_specs=(vmem,) * len(shapes),
         name="split",
     )(*arrays)
 
@@ -303,11 +342,13 @@
 
 
 def local(queries, keys, values, block_index, block_count, head_order):
-    kv_sent = split(split_kv_kernel, (8, 2, 64, HD), keys, values)
+    (kv_sent,) = split(split_kv_kernel, [(8, 2, 64, HD)], keys, values)
     kv_got = lax.all_to_all(kv_sent, ("zhi", "zlo"), split_axis=0, concat_axis=0, tiled=True)
+    (q_sent,) = split(split_q_kernel, [(H, 64, HD)], queries)
+    plan = tables(block_index, block_count)
+    kv_got, q_sent, (ready, arriving) = lax.optimization_barrier((kv_got, q_sent, plan))
     low, high = kv_got[:4], kv_got[4:]
     low_next, high_next = partner(low, "x", 1), partner(high, "y", 1)
-    q_sent = split(split_q_kernel, (H, 64, HD), queries)
     q_own = lax.all_to_all(
         q_sent.reshape(4, GROUP * 64, HD), "zhi", split_axis=0, concat_axis=0, tiled=True
     ).reshape(TILES, 64, HD)
@@ -322,7 +363,6 @@
             partner(jnp.concatenate([one, one_next]), outer, 3),
             partner(jnp.concatenate([two, two_next]), outer, 1),
         ]
-    ready, arriving = tables(block_index, block_count)
     *state, turned = attend(*ready, [q_own, q_oth], early, None)
     mine, others = attend(*arriving, [turned], late, state)
     attended = merge(mine, swap_cores(others))

time: 114 us -> 115 us (level)
  blocking collectives: 21.7 us -> 0 us
  waiting for transfers between devices: 14.5 us -> 27.5 us
  starting transfers between devices: 27.3 us -> 38.1 us
  Pallas kernels: 37.6 us -> 35.6 us
    all_to_all x1 -> x0, blocking collectives: 21.7 us -> none  [local(): lax.all_to_all(attended.reshape(4, GROUP * 64, HD), 'zhi', split_axis=0,...]
    all_to_all x0 -> x1, waiting for transfers between devices: none -> 15 us  [local(): lax.all_to_all(attended.reshape(4, GROUP * 64, HD), 'zhi', split_axis=0,...]
    all_to_all x0 -> x1, starting transfers between devices: none -> 8.2 us  [local(): lax.all_to_all(attended.reshape(4, GROUP * 64, HD), 'zhi', split_axis=0,...]
    all_to_all x1, waiting for transfers between devices: 7.13 us -> 4.35 us  [local(): lax.all_to_all(kv_sent, ('zhi', 'zlo'), split_axis=0, concat_axis=0, tile...]
    ppermute x14, starting transfers between devices: 15.3 us -> 17.9 us  [partner(): lax.ppermute(array, axis, [(i, i ^ mask) for i in range(lax.axis_size(axi...]
    pallas_call x2, Pallas kernels: 29.5 us -> 27.5 us  [attend(): pl.pallas_call(partial(attend_kernel, state is None, len(pieces)), out_sh...]
    unnamed x14 -> x18, local copies, waits for them, and re-layouts: 2.35 us -> 3.48 us
  transfers between devices with their start and end apart: 16 -> 17, of which waited for: 6 -> 6; matrix products, arithmetic and copies ran while one was open for 7% -> 8% of each run, Pallas kernels for 14% -> 13%
where the time goes in v1:
time: 115 us; the launch traced here: 114 us
  starting transfers between devices  38.1 us (33%)
  Pallas kernels  35.6 us (31%)
  waiting for transfers between devices  27.5 us (24%)
  other arithmetic  7.09 us (6%)
  local copies, waits for them, and re-layouts  4.88 us (4%)
    pallas_call x2, Pallas kernels, attend(): pl.pallas_call(partial(attend_kernel, state is None, len(pieces)), out_sh...  27.5 us
    ppermute x14, starting transfers between devices, partner(): lax.ppermute(array, axis, [(i, i ^ mask) for i in range(lax.axis_size(axi...  17.9 us
    all_to_all x1, waiting for transfers between devices, local(): lax.all_to_all(attended.reshape(4, GROUP * 64, HD), 'zhi', split_axis=0,...  15 us
    all_to_all x1, starting transfers between devices, local(): lax.all_to_all(kv_sent, ('zhi', 'zlo'), split_axis=0, concat_axis=0, tile...  8.57 us
    all_to_all x1, starting transfers between devices, local(): lax.all_to_all(attended.reshape(4, GROUP * 64, HD), 'zhi', split_axis=0,...  8.2 us
    ppermute x14, waiting for transfers between devices, partner(): lax.ppermute(array, axis, [(i, i ^ mask) for i in range(lax.axis_size(axi...  8.16 us
    all_to_all x1, waiting for transfers between devices, local(): lax.all_to_all(kv_sent, ('zhi', 'zlo'), split_axis=0, concat_axis=0, tile...  4.35 us
    pallas_call x2, Pallas kernels, split(): pl.pallas_call(kernel, out_shape=tuple((jax.ShapeDtypeStruct(shape, jnp.b...  3.6 us
  transfers between devices with their start and end apart: 17, of which 6 were waited for; matrix products, arithmetic and copies ran while one was open for 8% of the time, Pallas kernels for 13%

profile of v1, /device:TPU:46, one launch (start us, length us, event | category | flops | bytes accessed | tf_op | source)
XLA Modules:
  0.0 113.9 jit_solution(1785911623185396382)
XLA Ops:
  0.0 1.7 %split.2 = bf16[8,2,64,128]{3,2,1,0:T(8,128)(2,1)} custom-call(bf16[64,512]{1,0:T(8,128)(2,1)} %keys.1, bf16[64,512]{1,0:T(8,128)(2,1)} %values.1), custom_call_target="tpu_custom_call" | custom-call | tf_op jit(solution)/shard_map/split/pallas_call | solution.py:295
  1.7 8.6 %all-to-all-start = ((bf16[8,2,64,128]{3,2,1,0:T(8,128)(2,1)}), bf16[8,2,64,128]{3,2,1,0:T(8,128)(2,1)S(1)}, u32[]{:S(2)}, u32[]{:S(2)}) async-start(bf16[8,2,64,128]{3,2,1,0:T(8,128)(2,1)} %split.2), calls=%async_computation | async-start | bytes 524288 | tf_op jit(solution)/shard_map/all_to_all | solution.py:346
  11.9 1.9 %split.3 = bf16[28,64,128]{2,1,0:T(8,128)(2,1)} custom-call(bf16[64,3584]{1,0:T(8,128)(2,1)} %queries.1), custom_call_target="tpu_custom_call" | custom-call | tf_op jit(solution)/shard_map/split/pallas_call | solution.py:295
  13.8 2.2 %select_reduce_fusion = (s32[28,128]{1,0:T(8,128)S(1)}, s32[28,128]{1,0:T(8,128)S(1)}) fusion(s32[28,128]{1,0:T(8,128)S(1)} %get-tuple-element.36, s32[28,128]{1,0:T(8,128)S(1)} %get-tuple-element.31, s32[28,128]{1,0:T(8,128)S(1)} %get-tuple-element.35), kind=kLoop, calls=%fused_computation | loop fusion | flops 2745344 | bytes 71680 | tf_op jit(solution)/shard_map/reduce_sum | solution.py:338
  16.4 4.4 %all-to-all-done = bf16[8,2,64,128]{3,2,1,0:T(8,128)(2,1)S(1)} async-done(((bf16[8,2,64,128]{3,2,1,0:T(8,128)(2,1)}), bf16[8,2,64,128]{3,2,1,0:T(8,128)(2,1)S(1)}, u32[]{:S(2)}, u32[]{:S(2)}) %all-to-all-start) | async-done | bytes 262176 | tf_op jit(solution)/shard_map/all_to_all | solution.py:346
  20.7 3.5 %all-to-all-start.1 = ((bf16[4,448,128]{2,1,0:T(8,128)(2,1)}), bf16[4,448,128]{2,1,0:T(8,128)(2,1)S(1)}, u32[]{:S(2)}, u32[]{:S(2)}) async-start(bf16[4,448,128]{2,1,0:T(8,128)(2,1)} %bitcast.15), calls=%async_computation.1 | async-start | bytes 917504 | tf_op jit(solution)/shard_map/all_to_all | solution.py:352
  25.6 3.7 %collective-permute-done.1 = bf16[4,2,64,128]{3,2,1,0:T(8,128)(2,1)S(1)} collective-permute-done((bf16[4,2,64,128]{3,2,1,0:T(8,128)(2,1)S(1)}, bf16[4,2,64,128]{3,2,1,0:T(8,128)(2,1)S(1)}, u32[]{:S(2)}, u32[]{:S(2)}) %collective-permute-start.1) | collective-permute-done | bytes 131104 | tf_op jit(solution)/shard_map/ppermute | solution.py:24
  30.6 2.2 %collective-permute-start.6 = (bf16[8,2,64,128]{3,2,1,0:T(8,128)(2,1)S(1)}, bf16[8,2,64,128]{3,2,1,0:T(8,128)(2,1)S(1)}, u32[]{:S(2)}, u32[]{:S(2)}) collective-permute-start(bf16[8,2,64,128]{3,2,1,0:T(8,128)(2,1)S(1)} %pad_maximum_fusion.5.refs_8_), channel_id=1, source_target_pairs={{0,12},{4,8},{8,4},{12,0},{1,13},{5,9},{9,5},{13,1},{2,14},{6,10},... | collective-permute-start | bytes 786440 | tf_op jit(solution)/shard_map/ppermute | solution.py:24
  32.7 2.0 %collective-permute-start.3 = (bf16[8,2,64,128]{3,2,1,0:T(8,128)(2,1)S(1)}, bf16[8,2,64,128]{3,2,1,0:T(8,128)(2,1)}, u32[]{:S(2)}, u32[]{:S(2)}) collective-permute-start(bf16[8,2,64,128]{3,2,1,0:T(8,128)(2,1)S(1)} %pad_maximum_fusion.4.refs_4_), channel_id=1, source_target_pairs={{0,4},{4,0},{8,12},{12,8},{1,5},{5,1},{9,13},{13,9},{2,6},{6,2},{1... | collective-permute-start | bytes 786440 | tf_op jit(solution)/shard_map/ppermute | solution.py:24
  34.7 1.4 %collective-permute-start.7 = (bf16[8,2,64,128]{3,2,1,0:T(8,128)(2,1)S(1)}, bf16[8,2,64,128]{3,2,1,0:T(8,128)(2,1)}, u32[]{:S(2)}, u32[]{:S(2)}) collective-permute-start(bf16[8,2,64,128]{3,2,1,0:T(8,128)(2,1)S(1)} %pad_maximum_fusion.5.refs_8_), channel_id=1, source_target_pairs={{0,16},{16,0},{32,48},{48,32},{1,17},{17,1},{33,49},{49,33},{2,18}... | collective-permute-start | bytes 786440 | tf_op jit(solution)/shard_map/ppermute | solution.py:24
  36.1 1.5 %collective-permute-done.2.refs_5_ = bf16[8,2,64,128]{3,2,1,0:T(8,128)(2,1)S(1)} collective-permute-done((bf16[8,2,64,128]{3,2,1,0:T(8,128)(2,1)S(1)}, bf16[8,2,64,128]{3,2,1,0:T(8,128)(2,1)S(1)}, u32[]{:S(2)}, u32[]{:S(2)}) %collective-permute-start.2) | collective-permute-done | bytes 262176 | tf_op jit(solution)/shard_map/ppermute | solution.py:24
  37.6 2.3 %collective-permute-start.4 = (bf16[8,2,64,128]{3,2,1,0:T(8,128)(2,1)S(1)}, bf16[8,2,64,128]{3,2,1,0:T(8,128)(2,1)}, u32[]{:S(2)}, u32[]{:S(2)}) collective-permute-start(bf16[8,2,64,128]{3,2,1,0:T(8,128)(2,1)S(1)} %collective-permute-done.2.refs_5_), channel_id=1, source_target_pairs={{0,12},{4,8},{8,4},{12,0},{1,13},{5,9},{9,5},{13,1},{2,14},{6,10},... | collective-permute-start | bytes 786440 | tf_op jit(solution)/shard_map/ppermute | solution.py:24
  39.9 1.7 %collective-permute-start.8 = (bf16[8,2,64,128]{3,2,1,0:T(8,128)(2,1)S(1)}, bf16[8,2,64,128]{3,2,1,0:T(8,128)(2,1)}, u32[]{:S(2)}, u32[]{:S(2)}) collective-permute-start(bf16[8,2,64,128]{3,2,1,0:T(8,128)(2,1)S(1)} %collective-permute-done.6.refs_9_), channel_id=1, source_target_pairs={{0,48},{16,32},{32,16},{48,0},{1,49},{17,33},{33,17},{49,1},{2,50}... | collective-permute-start | bytes 786440 | tf_op jit(solution)/shard_map/ppermute | solution.py:24
  41.6 1.1 pad_maximum_fusion
  42.7 1.7 %collective-permute-start.9 = (bf16[16,2,64,128]{3,2,1,0:T(8,128)(2,1)S(1)}, bf16[16,2,64,128]{3,2,1,0:T(8,128)(2,1)S(1)}, u32[]{:S(2)}, u32[]{:S(2)}) collective-permute-start(bf16[16,2,64,128]{3,2,1,0:T(8,128)(2,1)S(1)} %pad_maximum_fusion), channel_id=1, source_target_pairs={{0,12},{4,8},{8,4},{12,0},{1,13},{5,9},{9,5},{13,1},{2,14},{6,10},... | collective-permute-start | bytes 1572872 | tf_op jit(solution)/shard_map/ppermute | solution.py:24
  45.4 1.3 %collective-permute-start.11 = (bf16[16,2,64,128]{3,2,1,0:T(8,128)(2,1)S(1)}, bf16[16,2,64,128]{3,2,1,0:T(8,128)(2,1)S(1)}, u32[]{:S(2)}, u32[]{:S(2)}) collective-permute-start(bf16[16,2,64,128]{3,2,1,0:T(8,128)(2,1)S(1)} %pad_maximum_fusion.2), channel_id=1, source_target_pairs={{0,48},{16,32},{32,16},{48,0},{1,49},{17,33},{33,17},{49,1},{2,50}... | collective-permute-start | bytes 1572872 | tf_op jit(solution)/shard_map/ppermute | solution.py:24
  47.8 3.4 %collective-permute-start.10 = (bf16[16,2,64,128]{3,2,1,0:T(8,128)(2,1)S(1)}, bf16[16,2,64,128]{3,2,1,0:T(8,128)(2,1)S(1)}, u32[]{:S(2)}, u32[]{:S(2)}) collective-permute-start(bf16[16,2,64,128]{3,2,1,0:T(8,128)(2,1)S(1)} %pad_maximum_fusion.1), channel_id=1, source_target_pairs={{0,4},{4,0},{8,12},{12,8},{1,5},{5,1},{9,13},{13,9},{2,6},{6,2},{1... | collective-permute-start | bytes 1572872 | tf_op jit(solution)/shard_map/ppermute | solution.py:24
  52.2 13.0 %attend.2 = (f32[29,8,128]{2,1,0:T(8,128)S(1)}, f32[29,8,128]{2,1,0:T(8,128)S(1)}, f32[29,128,128]{2,1,0:T(8,128)S(1)}, bf16[28,128,128]{2,1,0:T(8,128)(2,1)S(1)}) custom-call(s32[29,128]{1,0:T(8,128)S(1)} %pad.14.refs_0_, s32[29]{0:T(128)S(1)} %pad.15.refs_1_, bf16[28,64,128]{2,1,0:T(8,128)(2,1)S(1)} %bitcast.13, ...), custom_call_target="tpu_custom_call" | custom-call | flops 15032385536 | bytes 2097152 | tf_op jit(solution)/shard_map/attend/pallas_call | solution.py:187
  65.7 14.5 %attend.3 = (f32[29,64,128]{2,1,0:T(8,128)S(1)}, f32[29,64,128]{2,1,0:T(8,128)S(1)}) custom-call(s32[29,128]{1,0:T(8,128)S(1)} %pad.16.refs_0_, s32[29]{0:T(128)S(1)} %pad.17.refs_1_, bf16[28,128,128]{2,1,0:T(8,128)(2,1)S(1)} %get-tuple-element.23.refs_2_, bf16[16,2,64,128]{3,2,1,0:T(8,128)(2,1)S(1)} %collective-permute-done.9.refs_3_, ...), custom_call_target="tpu_custom_call" | custom-call | flops 15032385536 | bytes 2097152 | tf_op jit(solution)/shard_map/attend/pallas_call | solution.py:187
  81.2 2.5 %collective-permute-done.13.b_far = f32[29,64,128]{2,1,0:T(8,128)S(1)} collective-permute-done((f32[29,64,128]{2,1,0:T(8,128)S(1)}, f32[29,64,128]{2,1,0:T(8,128)S(1)}, u32[]{:S(2)}, u32[]{:S(2)}) %collective-permute-start.13) | collective-permute-done | bytes 950304 | tf_op jit(solution)/shard_map/ppermute | solution.py:24
  84.7 2.7 %merge.1 = bf16[28,64,128]{2,1,0:T(8,128)(2,1)} custom-call(f32[29,64,128]{2,1,0:T(8,128)} %copy-done.1, f32[29,64,128]{2,1,0:T(8,128)} %copy-done.4), custom_call_target="tpu_custom_call" | custom-call | tf_op jit(solution)/shard_map/merge/pallas_call | solution.py:248
  87.3 8.2 %all-to-all-start.2 = ((bf16[4,448,128]{2,1,0:T(8,128)(2,1)}), bf16[4,448,128]{2,1,0:T(8,128)(2,1)S(1)}, u32[]{:S(2)}, u32[]{:S(2)}) async-start(bf16[4,448,128]{2,1,0:T(8,128)(2,1)} %bitcast.14), calls=%async_computation.2 | async-start | bytes 917504 | tf_op jit(solution)/shard_map/all_to_all | solution.py:369
  96.2 15.0 %all-to-all-done.2 = bf16[4,448,128]{2,1,0:T(8,128)(2,1)S(1)} async-done(((bf16[4,448,128]{2,1,0:T(8,128)(2,1)}), bf16[4,448,128]{2,1,0:T(8,128)(2,1)S(1)}, u32[]{:S(2)}, u32[]{:S(2)}) %all-to-all-start.2) | async-done | bytes 458784 | tf_op jit(solution)/shard_map/all_to_all | solution.py:369
  112.0 1.9 %place.1 = bf16[64,3584]{1,0:T(8,128)(2,1)} custom-call(s32[28]{0:T(128)} %select_reduce_fusion.2.spot, bf16[28,64,128]{2,1,0:T(8,128)(2,1)} %bitcast.16), custom_call_target="tpu_custom_call" | custom-call | tf_op jit(solution)/shard_map/place/pallas_call | solution.py:269
  (57 shorter events, 11.6 us)
Async XLA Ops:
  0.0 10.3 %copy-start = (s32[128,28,128]{2,0,1:T(8,128)S(1)}, s32[128,28,128]{2,0,1:T(8,128)}, u32[]{:S(2)}) copy-start(s32[128,28,128]{2,0,1:T(8,128)} %param.9) | copy-start | bytes 5505028
  1.7 19.0 %all-to-all-start = ((bf16[8,2,64,128]{3,2,1,0:T(8,128)(2,1)}), bf16[8,2,64,128]{3,2,1,0:T(8,128)(2,1)S(1)}, u32[]{:S(2)}, u32[]{:S(2)}) async-start(bf16[8,2,64,128]{3,2,1,0:T(8,128)(2,1)} %split.2), calls=%async_computation | async-start | bytes 524288 | tf_op jit(solution)/shard_map/all_to_all | solution.py:346
  20.7 20.9 %all-to-all-start.1 = ((bf16[4,448,128]{2,1,0:T(8,128)(2,1)}), bf16[4,448,128]{2,1,0:T(8,128)(2,1)S(1)}, u32[]{:S(2)}, u32[]{:S(2)}) async-start(bf16[4,448,128]{2,1,0:T(8,128)(2,1)} %bitcast.15), calls=%async_computation.1 | async-start | bytes 917504 | tf_op jit(solution)/shard_map/all_to_all | solution.py:352
  24.2 5.1 %copy-start.3 = (bf16[4,2,64,128]{3,2,1,0:T(8,128)(2,1)}, bf16[4,2,64,128]{3,2,1,0:T(8,128)(2,1)S(1)}, u32[]{:S(2)}) copy-start(bf16[4,2,64,128]{3,2,1,0:T(8,128)(2,1)S(1)} %get-tuple-element.34) | copy-start | bytes 393220
  24.2 5.1 %collective-permute-start.1 = (bf16[4,2,64,128]{3,2,1,0:T(8,128)(2,1)S(1)}, bf16[4,2,64,128]{3,2,1,0:T(8,128)(2,1)S(1)}, u32[]{:S(2)}, u32[]{:S(2)}) collective-permute-start(bf16[4,2,64,128]{3,2,1,0:T(8,128)(2,1)S(1)} %get-tuple-element.34), channel_id=1, source_target_pairs={{0,16},{16,0},{32,48},{48,32},{1,17},{17,1},{33,49},{49,33},{2,18}... | collective-permute-start | bytes 393224 | tf_op jit(solution)/shard_map/ppermute | solution.py:24
  25.2 5.4 %collective-permute-start.5 = (bf16[4,2,64,128]{3,2,1,0:T(8,128)(2,1)S(1)}, bf16[4,2,64,128]{3,2,1,0:T(8,128)(2,1)S(1)}, u32[]{:S(2)}, u32[]{:S(2)}) collective-permute-start(bf16[4,2,64,128]{3,2,1,0:T(8,128)(2,1)S(1)} %get-tuple-element.33), channel_id=1, source_target_pairs={{0,4},{4,0},{8,12},{12,8},{1,5},{5,1},{9,13},{13,9},{2,6},{6,2},{1... | collective-permute-start | bytes 393224 | tf_op jit(solution)/shard_map/ppermute | solution.py:24
  30.0 7.7 %collective-permute-start.2 = (bf16[8,2,64,128]{3,2,1,0:T(8,128)(2,1)S(1)}, bf16[8,2,64,128]{3,2,1,0:T(8,128)(2,1)S(1)}, u32[]{:S(2)}, u32[]{:S(2)}) collective-permute-start(bf16[8,2,64,128]{3,2,1,0:T(8,128)(2,1)S(1)} %pad_maximum_fusion.4.refs_4_), channel_id=1, source_target_pairs={{0,48},{16,32},{32,16},{48,0},{1,49},{17,33},{33,17},{49,1},{2,50}... | collective-permute-start | bytes 786440 | tf_op jit(solution)/shard_map/ppermute | solution.py:24
  30.5 9.4 %copy-start.5 = (bf16[4,2,64,128]{3,2,1,0:T(8,128)(2,1)}, bf16[4,2,64,128]{3,2,1,0:T(8,128)(2,1)S(1)}, u32[]{:S(2)}) copy-start(bf16[4,2,64,128]{3,2,1,0:T(8,128)(2,1)S(1)} %collective-permute-done.5) | copy-start | bytes 393220
  30.6 9.3 %collective-permute-start.6 = (bf16[8,2,64,128]{3,2,1,0:T(8,128)(2,1)S(1)}, bf16[8,2,64,128]{3,2,1,0:T(8,128)(2,1)S(1)}, u32[]{:S(2)}, u32[]{:S(2)}) collective-permute-start(bf16[8,2,64,128]{3,2,1,0:T(8,128)(2,1)S(1)} %pad_maximum_fusion.5.refs_8_), channel_id=1, source_target_pairs={{0,12},{4,8},{8,4},{12,0},{1,13},{5,9},{9,5},{13,1},{2,14},{6,10},... | collective-permute-start | bytes 786440 | tf_op jit(solution)/shard_map/ppermute | solution.py:24
  32.7 8.9 %collective-permute-start.3 = (bf16[8,2,64,128]{3,2,1,0:T(8,128)(2,1)S(1)}, bf16[8,2,64,128]{3,2,1,0:T(8,128)(2,1)}, u32[]{:S(2)}, u32[]{:S(2)}) collective-permute-start(bf16[8,2,64,128]{3,2,1,0:T(8,128)(2,1)S(1)} %pad_maximum_fusion.4.refs_4_), channel_id=1, source_target_pairs={{0,4},{4,0},{8,12},{12,8},{1,5},{5,1},{9,13},{13,9},{2,6},{6,2},{1... | collective-permute-start | bytes 786440 | tf_op jit(solution)/shard_map/ppermute | solution.py:24
  34.7 9.7 %collective-permute-start.7 = (bf16[8,2,64,128]{3,2,1,0:T(8,128)(2,1)S(1)}, bf16[8,2,64,128]{3,2,1,0:T(8,128)(2,1)}, u32[]{:S(2)}, u32[]{:S(2)}) collective-permute-start(bf16[8,2,64,128]{3,2,1,0:T(8,128)(2,1)S(1)} %pad_maximum_fusion.5.refs_8_), channel_id=1, source_target_pairs={{0,16},{16,0},{32,48},{48,32},{1,17},{17,1},{33,49},{49,33},{2,18}... | collective-permute-start | bytes 786440 | tf_op jit(solution)/shard_map/ppermute | solution.py:24
  37.6 9.1 %collective-permute-start.4 = (bf16[8,2,64,128]{3,2,1,0:T(8,128)(2,1)S(1)}, bf16[8,2,64,128]{3,2,1,0:T(8,128)(2,1)}, u32[]{:S(2)}, u32[]{:S(2)}) collective-permute-start(bf16[8,2,64,128]{3,2,1,0:T(8,128)(2,1)S(1)} %collective-permute-done.2.refs_5_), channel_id=1, source_target_pairs={{0,12},{4,8},{8,4},{12,0},{1,13},{5,9},{9,5},{13,1},{2,14},{6,10},... | collective-permute-start | bytes 786440 | tf_op jit(solution)/shard_map/ppermute | solution.py:24
  39.9 11.2 %collective-permute-start.8 = (bf16[8,2,64,128]{3,2,1,0:T(8,128)(2,1)S(1)}, bf16[8,2,64,128]{3,2,1,0:T(8,128)(2,1)}, u32[]{:S(2)}, u32[]{:S(2)}) collective-permute-start(bf16[8,2,64,128]{3,2,1,0:T(8,128)(2,1)S(1)} %collective-permute-done.6.refs_9_), channel_id=1, source_target_pairs={{0,48},{16,32},{32,16},{48,0},{1,49},{17,33},{33,17},{49,1},{2,50}... | collective-permute-start | bytes 786440 | tf_op jit(solution)/shard_map/ppermute | solution.py:24
  41.6 10.6 %collective-permute-start = (bf16[28,64,128]{2,1,0:T(8,128)(2,1)S(1)}, bf16[28,64,128]{2,1,0:T(8,128)(2,1)S(1)}, u32[]{:S(2)}, u32[]{:S(2)}) collective-permute-start(bf16[28,64,128]{2,1,0:T(8,128)(2,1)S(1)} %bitcast.12), channel_id=1, source_target_pairs={{0,1},{1,0},{2,3},{3,2},{4,5},{5,4},{6,7},{7,6},{8,9},{9,8},{10,11... | collective-permute-start | bytes 1376264 | tf_op jit(solution)/shard_map/ppermute | solution.py:24
  42.7 22.6 %collective-permute-start.9 = (bf16[16,2,64,128]{3,2,1,0:T(8,128)(2,1)S(1)}, bf16[16,2,64,128]{3,2,1,0:T(8,128)(2,1)S(1)}, u32[]{:S(2)}, u32[]{:S(2)}) collective-permute-start(bf16[16,2,64,128]{3,2,1,0:T(8,128)(2,1)S(1)} %pad_maximum_fusion), channel_id=1, source_target_pairs={{0,12},{4,8},{8,4},{12,0},{1,13},{5,9},{9,5},{13,1},{2,14},{6,10},... | collective-permute-start | bytes 1572872 | tf_op jit(solution)/shard_map/ppermute | solution.py:24
  45.4 19.9 %collective-permute-start.11 = (bf16[16,2,64,128]{3,2,1,0:T(8,128)(2,1)S(1)}, bf16[16,2,64,128]{3,2,1,0:T(8,128)(2,1)S(1)}, u32[]{:S(2)}, u32[]{:S(2)}) collective-permute-start(bf16[16,2,64,128]{3,2,1,0:T(8,128)(2,1)S(1)} %pad_maximum_fusion.2), channel_id=1, source_target_pairs={{0,48},{16,32},{32,16},{48,0},{1,49},{17,33},{33,17},{49,1},{2,50}... | collective-permute-start | bytes 1572872 | tf_op jit(solution)/shard_map/ppermute | solution.py:24
  47.8 17.5 %collective-permute-start.10 = (bf16[16,2,64,128]{3,2,1,0:T(8,128)(2,1)S(1)}, bf16[16,2,64,128]{3,2,1,0:T(8,128)(2,1)S(1)}, u32[]{:S(2)}, u32[]{:S(2)}) collective-permute-start(bf16[16,2,64,128]{3,2,1,0:T(8,128)(2,1)S(1)} %pad_maximum_fusion.1), channel_id=1, source_target_pairs={{0,4},{4,0},{8,12},{12,8},{1,5},{5,1},{9,13},{13,9},{2,6},{6,2},{1... | collective-permute-start | bytes 1572872 | tf_op jit(solution)/shard_map/ppermute | solution.py:24
  52.1 13.6 %collective-permute-start.12 = (bf16[16,2,64,128]{3,2,1,0:T(8,128)(2,1)S(1)}, bf16[16,2,64,128]{3,2,1,0:T(8,128)(2,1)S(1)}, u32[]{:S(2)}, u32[]{:S(2)}) collective-permute-start(bf16[16,2,64,128]{3,2,1,0:T(8,128)(2,1)S(1)} %pad_maximum_fusion.3), channel_id=1, source_target_pairs={{0,16},{16,0},{32,48},{48,32},{1,17},{17,1},{33,49},{49,33},{2,18}... | collective-permute-start | bytes 1572872 | tf_op jit(solution)/shard_map/ppermute | solution.py:24
  80.2 0.9 copy-start.1
  81.2 14.4 %copy-start.7 = (s32[28]{0:T(128)S(1)}, s32[28]{0:T(128)}, u32[]{:S(2)}) copy-start(s32[28]{0:T(128)} %param.11) | copy-start | bytes 340
  81.2 2.5 %collective-permute-start.13 = (f32[29,64,128]{2,1,0:T(8,128)S(1)}, f32[29,64,128]{2,1,0:T(8,128)S(1)}, u32[]{:S(2)}, u32[]{:S(2)}) collective-permute-start(f32[29,64,128]{2,1,0:T(8,128)S(1)} %get-tuple-element.28), channel_id=1, source_target_pairs={{0,1},{1,0},{2,3},{3,2},{4,5},{5,4},{6,7},{7,6},{8,9},{9,8},{10,11... | collective-permute-start | bytes 2850824 | tf_op jit(solution)/shard_map/ppermute | solution.py:24
  83.7 1.0 copy-start.4
  87.3 23.9 %all-to-all-start.2 = ((bf16[4,448,128]{2,1,0:T(8,128)(2,1)}), bf16[4,448,128]{2,1,0:T(8,128)(2,1)S(1)}, u32[]{:S(2)}, u32[]{:S(2)}) async-start(bf16[4,448,128]{2,1,0:T(8,128)(2,1)} %bitcast.14), calls=%async_computation.2 | async-start | bytes 917504 | tf_op jit(solution)/shard_map/all_to_all | solution.py:369
  111.2 0.8 copy-start.2
  (1 other events, 0.7 us)

commit v2 on v1

--- a/solution.py
+++ b/solution.py
@@ -49,6 +49,7 @@
     lse, whole_out = (None, None) if first else take(2)
     (sem,) = refs
     core = lax.axis_index("core")
+    unroll = 12 if first else 16
     started, at = [], 0
     for source in sources:
         started.append(pltpu.make_async_copy(source, kv.at[pl.ds(at, source.shape[0])], sem))
@@ -94,7 +95,8 @@
             part = s[j * 64:(j + 1) * 64]
             top = jnp.max(part.reshape(8, 8, BLOCK), axis=0)
             tops.append(jnp.where((left_over > j) & ((d != j) | (left_over > NB)) if first else left_over > j, top, FLOOR))
-            s_ref[j * 64:(j + 1) * 64] = jnp.where(left_over > j, part, FLOOR)
+            cap = jnp.where(left_over > j, -FLOOR, FLOOR)
+            s_ref[j * 64:(j + 1) * 64] = jnp.minimum(part, cap)
         if first:
             here = pl.ds(pl.multiple_of(d * 64, 64), 64)
             part = jnp.where(seen | (left_over > NB), s_ref[here, :], FLOOR)
@@ -124,9 +126,9 @@
 
     def steps(_, carry):
         items = list(carry)
-        for k in range(8):
+        for k in range(unroll):
             t, c = items[0], items[1]
-            old = (k - 3) % 8
+            old = (k - 3) % unroll
             products(t, c, s_bufs[k % 4], m_bufs[k % 4], a_bufs[k % 4])
             weigh(items[6], items[7], s_bufs[old % 4], m_bufs[old % 4], a_bufs[old % 4])
             last = c + 1 >= chunks_of(t)
@@ -137,7 +139,7 @@
         return tuple(items)
 
     zero, dummy = jnp.int32(0), jnp.int32(TILES)
-    lax.fori_loop(0, (total + 10) // 8, steps, (zero, zero) + (dummy, zero) * 3)
+    lax.fori_loop(0, (total + 2 + unroll) // unroll, steps, (zero, zero) + (dummy, zero) * 3)
     if first:
         return
     lse[...] = jnp.zeros_like(lse)
@@ -226,12 +228,10 @@
         if i == 0:
             top = jnp.maximum(a[TILES], b[TILES])
             w_a = jnp.exp2(a[TILES] - top)
-            w_b = jnp.exp2(b[TILES] - top)
-            w_a = w_a / (w_a + w_b)
-            w_b = 1.0 - w_a
+            w_a = w_a / (w_a + jnp.exp2(b[TILES] - top))
             continue
         for t in range(at, at + count):
-            out[t] = (a[t] * w_a[:, t:t + 1] + b[t] * w_b[:, t:t + 1]).astype(jnp.bfloat16)
+            out[t] = (b[t] + (a[t] - b[t]) * w_a[:, t:t + 1]).astype(jnp.bfloat16)
         leaving.append(
             pltpu.make_async_copy(
                 out.at[pl.ds(at, count)], out_far.at[pl.ds(at, count)], sems.at[9 + i]

time: 115 us -> 115 us (level)
  Pallas kernels: 35.6 us -> 19.6 us
  starting transfers between devices: 38.1 us -> 47.2 us
  waiting for transfers between devices: 27.5 us -> 34.9 us
    pallas_call x2, Pallas kernels: 27.5 us -> 11.7 us  [attend(): pl.pallas_call(partial(attend_kernel, state is None, len(pieces)), out_sh...]
    all_to_all x1, starting transfers between devices: 8.2 us -> 17.3 us  [local(): lax.all_to_all(attended.reshape(4, GROUP * 64, HD), 'zhi', split_axis=0,...]
    ppermute x14, waiting for transfers between devices: 8.16 us -> 15.6 us  [partner(): lax.ppermute(array, axis, [(i, i ^ mask) for i in range(lax.axis_size(axi...]
  transfers between devices with their start and end apart: 17 -> 17, of which waited for: 6 -> 8; matrix products, arithmetic and copies ran while one was open for 8% -> 8% of each run, Pallas kernels for 13% -> 7%
where the time goes in v2:
time: 115 us; the launch traced here: 114 us
  starting transfers between devices  47.2 us (41%)
  waiting for transfers between devices  34.9 us (30%)
  Pallas kernels  19.6 us (17%)
  other arithmetic  7.09 us (6%)
  local copies, waits for them, and re-layouts  4.88 us (4%)
    ppermute x14, starting transfers between devices, partner(): lax.ppermute(array, axis, [(i, i ^ mask) for i in range(lax.axis_size(axi...  17.9 us
    all_to_all x1, starting transfers between devices, local(): lax.all_to_all(attended.reshape(4, GROUP * 64, HD), 'zhi', split_axis=0,...  17.3 us
    ppermute x14, waiting for transfers between devices, partner(): lax.ppermute(array, axis, [(i, i ^ mask) for i in range(lax.axis_size(axi...  15.6 us
    all_to_all x1, waiting for transfers between devices, local(): lax.all_to_all(attended.reshape(4, GROUP * 64, HD), 'zhi', split_axis=0,...  15 us
    pallas_call x2, Pallas kernels, attend(): pl.pallas_call(partial(attend_kernel, state is None, len(pieces)), out_sh...  11.7 us
    all_to_all x1, starting transfers between devices, local(): lax.all_to_all(kv_sent, ('zhi', 'zlo'), split_axis=0, concat_axis=0, tile...  8.57 us
    all_to_all x1, waiting for transfers between devices, local(): lax.all_to_all(kv_sent, ('zhi', 'zlo'), split_axis=0, concat_axis=0, tile...  4.35 us
    pallas_call x2, Pallas kernels, split(): pl.pallas_call(kernel, out_shape=tuple((jax.ShapeDtypeStruct(shape, jnp.b...  3.6 us
  transfers between devices with their start and end apart: 17, of which 8 were waited for; matrix products, arithmetic and copies ran while one was open for 8% of the time, Pallas kernels for 7%

profile of v2, /device:TPU:46, one launch (start us, length us, event | category | flops | bytes accessed | tf_op | source)
XLA Modules:
  0.0 114.3 jit_solution(14725150105568875678)
XLA Ops:
  0.0 1.7 %split.2 = bf16[8,2,64,128]{3,2,1,0:T(8,128)(2,1)} custom-call(bf16[64,512]{1,0:T(8,128)(2,1)} %keys.1, bf16[64,512]{1,0:T(8,128)(2,1)} %values.1), custom_call_target="tpu_custom_call" | custom-call | tf_op jit(solution)/shard_map/split/pallas_call | solution.py:295
  1.7 8.6 %all-to-all-start = ((bf16[8,2,64,128]{3,2,1,0:T(8,128)(2,1)}), bf16[8,2,64,128]{3,2,1,0:T(8,128)(2,1)S(1)}, u32[]{:S(2)}, u32[]{:S(2)}) async-start(bf16[8,2,64,128]{3,2,1,0:T(8,128)(2,1)} %split.2), calls=%async_computation | async-start | bytes 524288 | tf_op jit(solution)/shard_map/all_to_all | solution.py:346
  11.9 1.9 %split.3 = bf16[28,64,128]{2,1,0:T(8,128)(2,1)} custom-call(bf16[64,3584]{1,0:T(8,128)(2,1)} %queries.1), custom_call_target="tpu_custom_call" | custom-call | tf_op jit(solution)/shard_map/split/pallas_call | solution.py:295
  13.8 2.2 %select_reduce_fusion = (s32[28,128]{1,0:T(8,128)S(1)}, s32[28,128]{1,0:T(8,128)S(1)}) fusion(s32[28,128]{1,0:T(8,128)S(1)} %get-tuple-element.36, s32[28,128]{1,0:T(8,128)S(1)} %get-tuple-element.31, s32[28,128]{1,0:T(8,128)S(1)} %get-tuple-element.35), kind=kLoop, calls=%fused_computation | loop fusion | flops 2745344 | bytes 71680 | tf_op jit(solution)/shard_map/reduce_sum | solution.py:338
  16.4 4.4 %all-to-all-done = bf16[8,2,64,128]{3,2,1,0:T(8,128)(2,1)S(1)} async-done(((bf16[8,2,64,128]{3,2,1,0:T(8,128)(2,1)}), bf16[8,2,64,128]{3,2,1,0:T(8,128)(2,1)S(1)}, u32[]{:S(2)}, u32[]{:S(2)}) %all-to-all-start) | async-done | bytes 262176 | tf_op jit(solution)/shard_map/all_to_all | solution.py:346
  20.7 3.5 %all-to-all-start.1 = ((bf16[4,448,128]{2,1,0:T(8,128)(2,1)}), bf16[4,448,128]{2,1,0:T(8,128)(2,1)S(1)}, u32[]{:S(2)}, u32[]{:S(2)}) async-start(bf16[4,448,128]{2,1,0:T(8,128)(2,1)} %bitcast.15), calls=%async_computation.1 | async-start | bytes 917504 | tf_op jit(solution)/shard_map/all_to_all | solution.py:352
  25.6 3.7 %collective-permute-done.1 = bf16[4,2,64,128]{3,2,1,0:T(8,128)(2,1)S(1)} collective-permute-done((bf16[4,2,64,128]{3,2,1,0:T(8,128)(2,1)S(1)}, bf16[4,2,64,128]{3,2,1,0:T(8,128)(2,1)S(1)}, u32[]{:S(2)}, u32[]{:S(2)}) %collective-permute-start.1) | collective-permute-done | bytes 131104 | tf_op jit(solution)/shard_map/ppermute | solution.py:24
  30.6 2.2 %collective-permute-start.6 = (bf16[8,2,64,128]{3,2,1,0:T(8,128)(2,1)S(1)}, bf16[8,2,64,128]{3,2,1,0:T(8,128)(2,1)S(1)}, u32[]{:S(2)}, u32[]{:S(2)}) collective-permute-start(bf16[8,2,64,128]{3,2,1,0:T(8,128)(2,1)S(1)} %pad_maximum_fusion.5.refs_8_), channel_id=1, source_target_pairs={{0,12},{4,8},{8,4},{12,0},{1,13},{5,9},{9,5},{13,1},{2,14},{6,10},... | collective-permute-start | bytes 786440 | tf_op jit(solution)/shard_map/ppermute | solution.py:24
  32.7 2.0 %collective-permute-start.3 = (bf16[8,2,64,128]{3,2,1,0:T(8,128)(2,1)S(1)}, bf16[8,2,64,128]{3,2,1,0:T(8,128)(2,1)}, u32[]{:S(2)}, u32[]{:S(2)}) collective-permute-start(bf16[8,2,64,128]{3,2,1,0:T(8,128)(2,1)S(1)} %pad_maximum_fusion.4.refs_4_), channel_id=1, source_target_pairs={{0,4},{4,0},{8,12},{12,8},{1,5},{5,1},{9,13},{13,9},{2,6},{6,2},{1... | collective-permute-start | bytes 786440 | tf_op jit(solution)/shard_map/ppermute | solution.py:24
  36.1 1.5 %collective-permute-done.2.refs_5_ = bf16[8,2,64,128]{3,2,1,0:T(8,128)(2,1)S(1)} collective-permute-done((bf16[8,2,64,128]{3,2,1,0:T(8,128)(2,1)S(1)}, bf16[8,2,64,128]{3,2,1,0:T(8,128)(2,1)S(1)}, u32[]{:S(2)}, u32[]{:S(2)}) %collective-permute-start.2) | collective-permute-done | bytes 262176 | tf_op jit(solution)/shard_map/ppermute | solution.py:24
  37.6 2.3 %collective-permute-start.4 = (bf16[8,2,64,128]{3,2,1,0:T(8,128)(2,1)S(1)}, bf16[8,2,64,128]{3,2,1,0:T(8,128)(2,1)}, u32[]{:S(2)}, u32[]{:S(2)}) collective-permute-start(bf16[8,2,64,128]{3,2,1,0:T(8,128)(2,1)S(1)} %collective-permute-done.2.refs_5_), channel_id=1, source_target_pairs={{0,12},{4,8},{8,4},{12,0},{1,13},{5,9},{9,5},{13,1},{2,14},{6,10},... | collective-permute-start | bytes 786440 | tf_op jit(solution)/shard_map/ppermute | solution.py:24
  39.9 1.7 %collective-permute-start.8 = (bf16[8,2,64,128]{3,2,1,0:T(8,128)(2,1)S(1)}, bf16[8,2,64,128]{3,2,1,0:T(8,128)(2,1)}, u32[]{:S(2)}, u32[]{:S(2)}) collective-permute-start(bf16[8,2,64,128]{3,2,1,0:T(8,128)(2,1)S(1)} %collective-permute-done.6.refs_9_), channel_id=1, source_target_pairs={{0,48},{16,32},{32,16},{48,0},{1,49},{17,33},{33,17},{49,1},{2,50}... | collective-permute-start | bytes 786440 | tf_op jit(solution)/shard_map/ppermute | solution.py:24
  42.7 1.7 %collective-permute-start.9 = (bf16[16,2,64,128]{3,2,1,0:T(8,128)(2,1)S(1)}, bf16[16,2,64,128]{3,2,1,0:T(8,128)(2,1)S(1)}, u32[]{:S(2)}, u32[]{:S(2)}) collective-permute-start(bf16[16,2,64,128]{3,2,1,0:T(8,128)(2,1)S(1)} %pad_maximum_fusion), channel_id=1, source_target_pairs={{0,12},{4,8},{8,4},{12,0},{1,13},{5,9},{9,5},{13,1},{2,14},{6,10},... | collective-permute-start | bytes 1572872 | tf_op jit(solution)/shard_map/ppermute | solution.py:24
  47.8 3.4 %collective-permute-start.10 = (bf16[16,2,64,128]{3,2,1,0:T(8,128)(2,1)S(1)}, bf16[16,2,64,128]{3,2,1,0:T(8,128)(2,1)S(1)}, u32[]{:S(2)}, u32[]{:S(2)}) collective-permute-start(bf16[16,2,64,128]{3,2,1,0:T(8,128)(2,1)S(1)} %pad_maximum_fusion.1), channel_id=1, source_target_pairs={{0,4},{4,0},{8,12},{12,8},{1,5},{5,1},{9,13},{13,9},{2,6},{6,2},{1... | collective-permute-start | bytes 1572872 | tf_op jit(solution)/shard_map/ppermute | solution.py:24
  52.2 5.6 %attend.2 = (f32[29,8,128]{2,1,0:T(8,128)S(1)}, f32[29,8,128]{2,1,0:T(8,128)S(1)}, f32[29,128,128]{2,1,0:T(8,128)S(1)}, bf16[28,128,128]{2,1,0:T(8,128)(2,1)S(1)}) custom-call(s32[29,128]{1,0:T(8,128)S(1)} %pad.14.refs_0_, s32[29]{0:T(128)S(1)} %pad.15.refs_1_, bf16[28,64,128]{2,1,0:T(8,128)(2,1)S(1)} %bitcast.13, ...), custom_call_target="tpu_custom_call" | custom-call | flops 15032385536 | bytes 2097152 | tf_op jit(solution)/shard_map/attend/pallas_call | solution.py:189
  57.9 2.9 %collective-permute-done.11.refs_5_ = bf16[16,2,64,128]{3,2,1,0:T(8,128)(2,1)S(1)} collective-permute-done((bf16[16,2,64,128]{3,2,1,0:T(8,128)(2,1)S(1)}, bf16[16,2,64,128]{3,2,1,0:T(8,128)(2,1)S(1)}, u32[]{:S(2)}, u32[]{:S(2)}) %collective-permute-start.11) | collective-permute-done | bytes 524320 | tf_op jit(solution)/shard_map/ppermute | solution.py:24
  60.8 2.4 %collective-permute-done.10.refs_4_ = bf16[16,2,64,128]{3,2,1,0:T(8,128)(2,1)S(1)} collective-permute-done((bf16[16,2,64,128]{3,2,1,0:T(8,128)(2,1)S(1)}, bf16[16,2,64,128]{3,2,1,0:T(8,128)(2,1)S(1)}, u32[]{:S(2)}, u32[]{:S(2)}) %collective-permute-start.10) | collective-permute-done | bytes 524320 | tf_op jit(solution)/shard_map/ppermute | solution.py:24
  63.2 2.6 %collective-permute-done.12.refs_6_ = bf16[16,2,64,128]{3,2,1,0:T(8,128)(2,1)S(1)} collective-permute-done((bf16[16,2,64,128]{3,2,1,0:T(8,128)(2,1)S(1)}, bf16[16,2,64,128]{3,2,1,0:T(8,128)(2,1)S(1)}, u32[]{:S(2)}, u32[]{:S(2)}) %collective-permute-start.12) | collective-permute-done | bytes 524320 | tf_op jit(solution)/shard_map/ppermute | solution.py:24
  65.7 6.1 %attend.3 = (f32[29,64,128]{2,1,0:T(8,128)S(1)}, f32[29,64,128]{2,1,0:T(8,128)S(1)}) custom-call(s32[29,128]{1,0:T(8,128)S(1)} %pad.16.refs_0_, s32[29]{0:T(128)S(1)} %pad.17.refs_1_, bf16[28,128,128]{2,1,0:T(8,128)(2,1)S(1)} %get-tuple-element.23.refs_2_, bf16[16,2,64,128]{3,2,1,0:T(8,128)(2,1)S(1)} %collective-permute-done.9.refs_3_, ...), custom_call_target="tpu_custom_call" | custom-call | flops 15032385536 | bytes 2097152 | tf_op jit(solution)/shard_map/attend/pallas_call | solution.py:189
  72.7 2.5 %collective-permute-done.13.b_far = f32[29,64,128]{2,1,0:T(8,128)S(1)} collective-permute-done((f32[29,64,128]{2,1,0:T(8,128)S(1)}, f32[29,64,128]{2,1,0:T(8,128)S(1)}, u32[]{:S(2)}, u32[]{:S(2)}) %collective-permute-start.13) | collective-permute-done | bytes 950304 | tf_op jit(solution)/shard_map/ppermute | solution.py:24
  76.2 2.5 %merge.1 = bf16[28,64,128]{2,1,0:T(8,128)(2,1)} custom-call(f32[29,64,128]{2,1,0:T(8,128)} %copy-done.1, f32[29,64,128]{2,1,0:T(8,128)} %copy-done.4), custom_call_target="tpu_custom_call" | custom-call | tf_op jit(solution)/shard_map/merge/pallas_call | solution.py:248
  78.7 17.3 %all-to-all-start.2 = ((bf16[4,448,128]{2,1,0:T(8,128)(2,1)}), bf16[4,448,128]{2,1,0:T(8,128)(2,1)S(1)}, u32[]{:S(2)}, u32[]{:S(2)}) async-start(bf16[4,448,128]{2,1,0:T(8,128)(2,1)} %bitcast.14), calls=%async_computation.2 | async-start | bytes 917504 | tf_op jit(solution)/shard_map/all_to_all | solution.py:369
  96.6 15.0 %all-to-all-done.2 = bf16[4,448,128]{2,1,0:T(8,128)(2,1)S(1)} async-done(((bf16[4,448,128]{2,1,0:T(8,128)(2,1)}), bf16[4,448,128]{2,1,0:T(8,128)(2,1)S(1)}, u32[]{:S(2)}, u32[]{:S(2)}) %all-to-all-start.2) | async-done | bytes 458784 | tf_op jit(solution)/shard_map/all_to_all | solution.py:369
  112.4 1.9 %place.1 = bf16[64,3584]{1,0:T(8,128)(2,1)} custom-call(s32[28]{0:T(128)} %select_reduce_fusion.2.spot, bf16[28,64,128]{2,1,0:T(8,128)(2,1)} %bitcast.16), custom_call_target="tpu_custom_call" | custom-call | tf_op jit(solution)/shard_map/place/pallas_call | solution.py:269
  (57 shorter events, 15.0 us)
Async XLA Ops:
  0.0 10.3 %copy-start = (s32[128,28,128]{2,0,1:T(8,128)S(1)}, s32[128,28,128]{2,0,1:T(8,128)}, u32[]{:S(2)}) copy-start(s32[128,28,128]{2,0,1:T(8,128)} %param.9) | copy-start | bytes 5505028
  1.7 19.0 %all-to-all-start = ((bf16[8,2,64,128]{3,2,1,0:T(8,128)(2,1)}), bf16[8,2,64,128]{3,2,1,0:T(8,128)(2,1)S(1)}, u32[]{:S(2)}, u32[]{:S(2)}) async-start(bf16[8,2,64,128]{3,2,1,0:T(8,128)(2,1)} %split.2), calls=%async_computation | async-start | bytes 524288 | tf_op jit(solution)/shard_map/all_to_all | solution.py:346
  20.7 20.9 %all-to-all-start.1 = ((bf16[4,448,128]{2,1,0:T(8,128)(2,1)}), bf16[4,448,128]{2,1,0:T(8,128)(2,1)S(1)}, u32[]{:S(2)}, u32[]{:S(2)}) async-start(bf16[4,448,128]{2,1,0:T(8,128)(2,1)} %bitcast.15), calls=%async_computation.1 | async-start | bytes 917504 | tf_op jit(solution)/shard_map/all_to_all | solution.py:352
  24.2 5.1 %copy-start.3 = (bf16[4,2,64,128]{3,2,1,0:T(8,128)(2,1)}, bf16[4,2,64,128]{3,2,1,0:T(8,128)(2,1)S(1)}, u32[]{:S(2)}) copy-start(bf16[4,2,64,128]{3,2,1,0:T(8,128)(2,1)S(1)} %get-tuple-element.34) | copy-start | bytes 393220
  24.2 5.1 %collective-permute-start.1 = (bf16[4,2,64,128]{3,2,1,0:T(8,128)(2,1)S(1)}, bf16[4,2,64,128]{3,2,1,0:T(8,128)(2,1)S(1)}, u32[]{:S(2)}, u32[]{:S(2)}) collective-permute-start(bf16[4,2,64,128]{3,2,1,0:T(8,128)(2,1)S(1)} %get-tuple-element.34), channel_id=1, source_target_pairs={{0,16},{16,0},{32,48},{48,32},{1,17},{17,1},{33,49},{49,33},{2,18}... | collective-permute-start | bytes 393224 | tf_op jit(solution)/shard_map/ppermute | solution.py:24
  25.2 5.4 %collective-permute-start.5 = (bf16[4,2,64,128]{3,2,1,0:T(8,128)(2,1)S(1)}, bf16[4,2,64,128]{3,2,1,0:T(8,128)(2,1)S(1)}, u32[]{:S(2)}, u32[]{:S(2)}) collective-permute-start(bf16[4,2,64,128]{3,2,1,0:T(8,128)(2,1)S(1)} %get-tuple-element.33), channel_id=1, source_target_pairs={{0,4},{4,0},{8,12},{12,8},{1,5},{5,1},{9,13},{13,9},{2,6},{6,2},{1... | collective-permute-start | bytes 393224 | tf_op jit(solution)/shard_map/ppermute | solution.py:24
  30.0 7.7 %collective-permute-start.2 = (bf16[8,2,64,128]{3,2,1,0:T(8,128)(2,1)S(1)}, bf16[8,2,64,128]{3,2,1,0:T(8,128)(2,1)S(1)}, u32[]{:S(2)}, u32[]{:S(2)}) collective-permute-start(bf16[8,2,64,128]{3,2,1,0:T(8,128)(2,1)S(1)} %pad_maximum_fusion.4.refs_4_), channel_id=1, source_target_pairs={{0,48},{16,32},{32,16},{48,0},{1,49},{17,33},{33,17},{49,1},{2,50}... | collective-permute-start | bytes 786440 | tf_op jit(solution)/shard_map/ppermute | solution.py:24
  30.5 9.4 %copy-start.5 = (bf16[4,2,64,128]{3,2,1,0:T(8,128)(2,1)}, bf16[4,2,64,128]{3,2,1,0:T(8,128)(2,1)S(1)}, u32[]{:S(2)}) copy-start(bf16[4,2,64,128]{3,2,1,0:T(8,128)(2,1)S(1)} %collective-permute-done.5) | copy-start | bytes 393220
  30.6 9.3 %collective-permute-start.6 = (bf16[8,2,64,128]{3,2,1,0:T(8,128)(2,1)S(1)}, bf16[8,2,64,128]{3,2,1,0:T(8,128)(2,1)S(1)}, u32[]{:S(2)}, u32[]{:S(2)}) collective-permute-start(bf16[8,2,64,128]{3,2,1,0:T(8,128)(2,1)S(1)} %pad_maximum_fusion.5.refs_8_), channel_id=1, source_target_pairs={{0,12},{4,8},{8,4},{12,0},{1,13},{5,9},{9,5},{13,1},{2,14},{6,10},... | collective-permute-start | bytes 786440 | tf_op jit(solution)/shard_map/ppermute | solution.py:24
  32.7 8.9 %collective-permute-start.3 = (bf16[8,2,64,128]{3,2,1,0:T(8,128)(2,1)S(1)}, bf16[8,2,64,128]{3,2,1,0:T(8,128)(2,1)}, u32[]{:S(2)}, u32[]{:S(2)}) collective-permute-start(bf16[8,2,64,128]{3,2,1,0:T(8,128)(2,1)S(1)} %pad_maximum_fusion.4.refs_4_), channel_id=1, source_target_pairs={{0,4},{4,0},{8,12},{12,8},{1,5},{5,1},{9,13},{13,9},{2,6},{6,2},{1... | collective-permute-start | bytes 786440 | tf_op jit(solution)/shard_map/ppermute | solution.py:24
  34.7 9.7 %collective-permute-start.7 = (bf16[8,2,64,128]{3,2,1,0:T(8,128)(2,1)S(1)}, bf16[8,2,64,128]{3,2,1,0:T(8,128)(2,1)}, u32[]{:S(2)}, u32[]{:S(2)}) collective-permute-start(bf16[8,2,64,128]{3,2,1,0:T(8,128)(2,1)S(1)} %pad_maximum_fusion.5.refs_8_), channel_id=1, source_target_pairs={{0,16},{16,0},{32,48},{48,32},{1,17},{17,1},{33,49},{49,33},{2,18}... | collective-permute-start | bytes 786440 | tf_op jit(solution)/shard_map/ppermute | solution.py:24
  37.6 9.1 %collective-permute-start.4 = (bf16[8,2,64,128]{3,2,1,0:T(8,128)(2,1)S(1)}, bf16[8,2,64,128]{3,2,1,0:T(8,128)(2,1)}, u32[]{:S(2)}, u32[]{:S(2)}) collective-permute-start(bf16[8,2,64,128]{3,2,1,0:T(8,128)(2,1)S(1)} %collective-permute-done.2.refs_5_), channel_id=1, source_target_pairs={{0,12},{4,8},{8,4},{12,0},{1,13},{5,9},{9,5},{13,1},{2,14},{6,10},... | collective-permute-start | bytes 786440 | tf_op jit(solution)/shard_map/ppermute | solution.py:24
  39.9 11.2 %collective-permute-start.8 = (bf16[8,2,64,128]{3,2,1,0:T(8,128)(2,1)S(1)}, bf16[8,2,64,128]{3,2,1,0:T(8,128)(2,1)}, u32[]{:S(2)}, u32[]{:S(2)}) collective-permute-start(bf16[8,2,64,128]{3,2,1,0:T(8,128)(2,1)S(1)} %collective-permute-done.6.refs_9_), channel_id=1, source_target_pairs={{0,48},{16,32},{32,16},{48,0},{1,49},{17,33},{33,17},{49,1},{2,50}... | collective-permute-start | bytes 786440 | tf_op jit(solution)/shard_map/ppermute | solution.py:24
  41.6 10.6 %collective-permute-start = (bf16[28,64,128]{2,1,0:T(8,128)(2,1)S(1)}, bf16[28,64,128]{2,1,0:T(8,128)(2,1)S(1)}, u32[]{:S(2)}, u32[]{:S(2)}) collective-permute-start(bf16[28,64,128]{2,1,0:T(8,128)(2,1)S(1)} %bitcast.12), channel_id=1, source_target_pairs={{0,1},{1,0},{2,3},{3,2},{4,5},{5,4},{6,7},{7,6},{8,9},{9,8},{10,11... | collective-permute-start | bytes 1376264 | tf_op jit(solution)/shard_map/ppermute | solution.py:24
  42.7 15.2 %collective-permute-start.9 = (bf16[16,2,64,128]{3,2,1,0:T(8,128)(2,1)S(1)}, bf16[16,2,64,128]{3,2,1,0:T(8,128)(2,1)S(1)}, u32[]{:S(2)}, u32[]{:S(2)}) collective-permute-start(bf16[16,2,64,128]{3,2,1,0:T(8,128)(2,1)S(1)} %pad_maximum_fusion), channel_id=1, source_target_pairs={{0,12},{4,8},{8,4},{12,0},{1,13},{5,9},{9,5},{13,1},{2,14},{6,10},... | collective-permute-start | bytes 1572872 | tf_op jit(solution)/shard_map/ppermute | solution.py:24
  45.4 15.4 %collective-permute-start.11 = (bf16[16,2,64,128]{3,2,1,0:T(8,128)(2,1)S(1)}, bf16[16,2,64,128]{3,2,1,0:T(8,128)(2,1)S(1)}, u32[]{:S(2)}, u32[]{:S(2)}) collective-permute-start(bf16[16,2,64,128]{3,2,1,0:T(8,128)(2,1)S(1)} %pad_maximum_fusion.2), channel_id=1, source_target_pairs={{0,48},{16,32},{32,16},{48,0},{1,49},{17,33},{33,17},{49,1},{2,50}... | collective-permute-start | bytes 1572872 | tf_op jit(solution)/shard_map/ppermute | solution.py:24
  47.8 15.4 %collective-permute-start.10 = (bf16[16,2,64,128]{3,2,1,0:T(8,128)(2,1)S(1)}, bf16[16,2,64,128]{3,2,1,0:T(8,128)(2,1)S(1)}, u32[]{:S(2)}, u32[]{:S(2)}) collective-permute-start(bf16[16,2,64,128]{3,2,1,0:T(8,128)(2,1)S(1)} %pad_maximum_fusion.1), channel_id=1, source_target_pairs={{0,4},{4,0},{8,12},{12,8},{1,5},{5,1},{9,13},{13,9},{2,6},{6,2},{1... | collective-permute-start | bytes 1572872 | tf_op jit(solution)/shard_map/ppermute | solution.py:24
  52.1 13.6 %collective-permute-start.12 = (bf16[16,2,64,128]{3,2,1,0:T(8,128)(2,1)S(1)}, bf16[16,2,64,128]{3,2,1,0:T(8,128)(2,1)S(1)}, u32[]{:S(2)}, u32[]{:S(2)}) collective-permute-start(bf16[16,2,64,128]{3,2,1,0:T(8,128)(2,1)S(1)} %pad_maximum_fusion.3), channel_id=1, source_target_pairs={{0,16},{16,0},{32,48},{48,32},{1,17},{17,1},{33,49},{49,33},{2,18}... | collective-permute-start | bytes 1572872 | tf_op jit(solution)/shard_map/ppermute | solution.py:24
  71.8 0.9 copy-start.1
  72.7 23.3 %copy-start.7 = (s32[28]{0:T(128)S(1)}, s32[28]{0:T(128)}, u32[]{:S(2)}) copy-start(s32[28]{0:T(128)} %param.11) | copy-start | bytes 340
  72.7 2.5 %collective-permute-start.13 = (f32[29,64,128]{2,1,0:T(8,128)S(1)}, f32[29,64,128]{2,1,0:T(8,128)S(1)}, u32[]{:S(2)}, u32[]{:S(2)}) collective-permute-start(f32[29,64,128]{2,1,0:T(8,128)S(1)} %get-tuple-element.28), channel_id=1, source_target_pairs={{0,1},{1,0},{2,3},{3,2},{4,5},{5,4},{6,7},{7,6},{8,9},{9,8},{10,11... | collective-permute-start | bytes 2850824 | tf_op jit(solution)/shard_map/ppermute | solution.py:24
  75.2 1.0 copy-start.4
  78.7 33.0 %all-to-all-start.2 = ((bf16[4,448,128]{2,1,0:T(8,128)(2,1)}), bf16[4,448,128]{2,1,0:T(8,128)(2,1)S(1)}, u32[]{:S(2)}, u32[]{:S(2)}) async-start(bf16[4,448,128]{2,1,0:T(8,128)(2,1)} %bitcast.14), calls=%async_computation.2 | async-start | bytes 917504 | tf_op jit(solution)/shard_map/all_to_all | solution.py:369
  111.7 0.8 copy-start.2
  (1 other events, 0.7 us)

commit v3 on v2

--- a/solution.py
+++ b/solution.py
@@ -144,11 +144,10 @@
         return
     lse[...] = jnp.zeros_like(lse)
 
-    def finish(t, _):
+    def finish(t):
         whole = jnp.sum(l_ref[t], axis=0, keepdims=True)
-        whole_out[t] = (acc[t] / whole).T
-        lse[pl.ds(t, 1), :] = m_ref[t][:1] * EXP_SCALE + jnp.log2(whole)
-        return 0
+        whole_out[t] = (acc[t] * (1.0 / whole)).T
+        lse[t:t + 1, :] = m_ref[t, :1] * EXP_SCALE + jnp.log2(whole)
 
     leaving = []
 
@@ -164,7 +163,8 @@
             leaving[-1].start()
 
     for stripe in range(4):
-        lax.fori_loop(stripe * GROUP, (stripe + 1) * GROUP, finish, 0, unroll=GROUP)
+        for t in range(stripe * GROUP, (stripe + 1) * GROUP):
+            finish(t)
         leave(stripe * GROUP, GROUP)
     whole_out[TILES] = lse[...].T
     leave(TILES, 1)

time: 115 us -> 114 us (level)
  Pallas kernels: 19.6 us -> 36.9 us
  starting transfers between devices: 47.2 us -> 35.9 us
  waiting for transfers between devices: 34.9 us -> 27.1 us
    pallas_call x2, Pallas kernels: 11.7 us -> 29 us  [attend(): pl.pallas_call(partial(attend_kernel, state is None, len(pieces)), out_sh...]
    all_to_all x1, starting transfers between devices: 17.3 us -> 6 us  [local(): lax.all_to_all(attended.reshape(4, GROUP * 64, HD), 'zhi', split_axis=0,...]
    ppermute x14, waiting for transfers between devices: 15.6 us -> 7.74 us  [partner(): lax.ppermute(array, axis, [(i, i ^ mask) for i in range(lax.axis_size(axi...]
  transfers between devices with their start and end apart: 17 -> 17, of which waited for: 8 -> 5; matrix products, arithmetic and copies ran while one was open for 8% -> 8% of each run, Pallas kernels for 7% -> 14%
where the time goes in v3:
time: 114 us; the launch traced here: 113 us
  Pallas kernels  36.9 us (32%)
  starting transfers between devices  35.9 us (31%)
  waiting for transfers between devices  27.1 us (24%)
  other arithmetic  7.09 us (6%)
  local copies, waits for them, and re-layouts  4.88 us (4%)
    pallas_call x2, Pallas kernels, attend(): pl.pallas_call(partial(attend_kernel, state is None, len(pieces)), out_sh...  29 us
    ppermute x14, starting transfers between devices, partner(): lax.ppermute(array, axis, [(i, i ^ mask) for i in range(lax.axis_size(axi...  17.9 us
    all_to_all x1, waiting for transfers between devices, local(): lax.all_to_all(attended.reshape(4, GROUP * 64, HD), 'zhi', split_axis=0,...  15 us
    all_to_all x1, starting transfers between devices, local(): lax.all_to_all(kv_sent, ('zhi', 'zlo'), split_axis=0, concat_axis=0, tile...  8.57 us
    ppermute x14, waiting for transfers between devices, partner(): lax.ppermute(array, axis, [(i, i ^ mask) for i in range(lax.axis_size(axi...  7.74 us
    all_to_all x1, starting transfers between devices, local(): lax.all_to_all(attended.reshape(4, GROUP * 64, HD), 'zhi', split_axis=0,...  6 us
    all_to_all x1, waiting for transfers between devices, local(): lax.all_to_all(kv_sent, ('zhi', 'zlo'), split_axis=0, concat_axis=0, tile...  4.35 us
    pallas_call x2, Pallas kernels, split(): pl.pallas_call(kernel, out_shape=tuple((jax.ShapeDtypeStruct(shape, jnp.b...  3.6 us
  transfers between devices with their start and end apart: 17, of which 5 were waited for; matrix products, arithmetic and copies ran while one was open for 8% of the time, Pallas kernels for 14%

profile of v3, /device:TPU:46, one launch (start us, length us, event | category | flops | bytes accessed | tf_op | source)
XLA Modules:
  0.0 112.5 jit_solution(733858284012578703)
XLA Ops:
  0.0 1.7 %split.2 = bf16[8,2,64,128]{3,2,1,0:T(8,128)(2,1)} custom-call(bf16[64,512]{1,0:T(8,128)(2,1)} %keys.1, bf16[64,512]{1,0:T(8,128)(2,1)} %values.1), custom_call_target="tpu_custom_call" | custom-call | tf_op jit(solution)/shard_map/split/pallas_call | solution.py:295
  1.7 8.6 %all-to-all-start = ((bf16[8,2,64,128]{3,2,1,0:T(8,128)(2,1)}), bf16[8,2,64,128]{3,2,1,0:T(8,128)(2,1)S(1)}, u32[]{:S(2)}, u32[]{:S(2)}) async-start(bf16[8,2,64,128]{3,2,1,0:T(8,128)(2,1)} %split.2), calls=%async_computation | async-start | bytes 524288 | tf_op jit(solution)/shard_map/all_to_all | solution.py:346
  11.9 1.9 %split.3 = bf16[28,64,128]{2,1,0:T(8,128)(2,1)} custom-call(bf16[64,3584]{1,0:T(8,128)(2,1)} %queries.1), custom_call_target="tpu_custom_call" | custom-call | tf_op jit(solution)/shard_map/split/pallas_call | solution.py:295
  13.8 2.2 %select_reduce_fusion = (s32[28,128]{1,0:T(8,128)S(1)}, s32[28,128]{1,0:T(8,128)S(1)}) fusion(s32[28,128]{1,0:T(8,128)S(1)} %get-tuple-element.36, s32[28,128]{1,0:T(8,128)S(1)} %get-tuple-element.31, s32[28,128]{1,0:T(8,128)S(1)} %get-tuple-element.35), kind=kLoop, calls=%fused_computation | loop fusion | flops 2745344 | bytes 71680 | tf_op jit(solution)/shard_map/reduce_sum | solution.py:338
  16.4 4.4 %all-to-all-done = bf16[8,2,64,128]{3,2,1,0:T(8,128)(2,1)S(1)} async-done(((bf16[8,2,64,128]{3,2,1,0:T(8,128)(2,1)}), bf16[8,2,64,128]{3,2,1,0:T(8,128)(2,1)S(1)}, u32[]{:S(2)}, u32[]{:S(2)}) %all-to-all-start) | async-done | bytes 262176 | tf_op jit(solution)/shard_map/all_to_all | solution.py:346
  20.7 3.5 %all-to-all-start.1 = ((bf16[4,448,128]{2,1,0:T(8,128)(2,1)}), bf16[4,448,128]{2,1,0:T(8,128)(2,1)S(1)}, u32[]{:S(2)}, u32[]{:S(2)}) async-start(bf16[4,448,128]{2,1,0:T(8,128)(2,1)} %bitcast.15), calls=%async_computation.1 | async-start | bytes 917504 | tf_op jit(solution)/shard_map/all_to_all | solution.py:352
  25.6 3.7 %collective-permute-done.1 = bf16[4,2,64,128]{3,2,1,0:T(8,128)(2,1)S(1)} collective-permute-done((bf16[4,2,64,128]{3,2,1,0:T(8,128)(2,1)S(1)}, bf16[4,2,64,128]{3,2,1,0:T(8,128)(2,1)S(1)}, u32[]{:S(2)}, u32[]{:S(2)}) %collective-permute-start.1) | collective-permute-done | bytes 131104 | tf_op jit(solution)/shard_map/ppermute | solution.py:24
  30.6 2.2 %collective-permute-start.6 = (bf16[8,2,64,128]{3,2,1,0:T(8,128)(2,1)S(1)}, bf16[8,2,64,128]{3,2,1,0:T(8,128)(2,1)S(1)}, u32[]{:S(2)}, u32[]{:S(2)}) collective-permute-start(bf16[8,2,64,128]{3,2,1,0:T(8,128)(2,1)S(1)} %pad_maximum_fusion.5.refs_8_), channel_id=1, source_target_pairs={{0,12},{4,8},{8,4},{12,0},{1,13},{5,9},{9,5},{13,1},{2,14},{6,10},... | collective-permute-start | bytes 786440 | tf_op jit(solution)/shard_map/ppermute | solution.py:24
  32.7 2.0 %collective-permute-start.3 = (bf16[8,2,64,128]{3,2,1,0:T(8,128)(2,1)S(1)}, bf16[8,2,64,128]{3,2,1,0:T(8,128)(2,1)}, u32[]{:S(2)}, u32[]{:S(2)}) collective-permute-start(bf16[8,2,64,128]{3,2,1,0:T(8,128)(2,1)S(1)} %pad_maximum_fusion.4.refs_4_), channel_id=1, source_target_pairs={{0,4},{4,0},{8,12},{12,8},{1,5},{5,1},{9,13},{13,9},{2,6},{6,2},{1... | collective-permute-start | bytes 786440 | tf_op jit(solution)/shard_map/ppermute | solution.py:24
  34.7 1.4 %collective-permute-start.7 = (bf16[8,2,64,128]{3,2,1,0:T(8,128)(2,1)S(1)}, bf16[8,2,64,128]{3,2,1,0:T(8,128)(2,1)}, u32[]{:S(2)}, u32[]{:S(2)}) collective-permute-start(bf16[8,2,64,128]{3,2,1,0:T(8,128)(2,1)S(1)} %pad_maximum_fusion.5.refs_8_), channel_id=1, source_target_pairs={{0,16},{16,0},{32,48},{48,32},{1,17},{17,1},{33,49},{49,33},{2,18}... | collective-permute-start | bytes 786440 | tf_op jit(solution)/shard_map/ppermute | solution.py:24
  36.1 1.5 %collective-permute-done.2.refs_5_ = bf16[8,2,64,128]{3,2,1,0:T(8,128)(2,1)S(1)} collective-permute-done((bf16[8,2,64,128]{3,2,1,0:T(8,128)(2,1)S(1)}, bf16[8,2,64,128]{3,2,1,0:T(8,128)(2,1)S(1)}, u32[]{:S(2)}, u32[]{:S(2)}) %collective-permute-start.2) | collective-permute-done | bytes 262176 | tf_op jit(solution)/shard_map/ppermute | solution.py:24
  37.6 2.3 %collective-permute-start.4 = (bf16[8,2,64,128]{3,2,1,0:T(8,128)(2,1)S(1)}, bf16[8,2,64,128]{3,2,1,0:T(8,128)(2,1)}, u32[]{:S(2)}, u32[]{:S(2)}) collective-permute-start(bf16[8,2,64,128]{3,2,1,0:T(8,128)(2,1)S(1)} %collective-permute-done.2.refs_5_), channel_id=1, source_target_pairs={{0,12},{4,8},{8,4},{12,0},{1,13},{5,9},{9,5},{13,1},{2,14},{6,10},... | collective-permute-start | bytes 786440 | tf_op jit(solution)/shard_map/ppermute | solution.py:24
  39.9 1.7 %collective-permute-start.8 = (bf16[8,2,64,128]{3,2,1,0:T(8,128)(2,1)S(1)}, bf16[8,2,64,128]{3,2,1,0:T(8,128)(2,1)}, u32[]{:S(2)}, u32[]{:S(2)}) collective-permute-start(bf16[8,2,64,128]{3,2,1,0:T(8,128)(2,1)S(1)} %collective-permute-done.6.refs_9_), channel_id=1, source_target_pairs={{0,48},{16,32},{32,16},{48,0},{1,49},{17,33},{33,17},{49,1},{2,50}... | collective-permute-start | bytes 786440 | tf_op jit(solution)/shard_map/ppermute | solution.py:24
  41.6 1.1 pad_maximum_fusion
  42.7 1.7 %collective-permute-start.9 = (bf16[16,2,64,128]{3,2,1,0:T(8,128)(2,1)S(1)}, bf16[16,2,64,128]{3,2,1,0:T(8,128)(2,1)S(1)}, u32[]{:S(2)}, u32[]{:S(2)}) collective-permute-start(bf16[16,2,64,128]{3,2,1,0:T(8,128)(2,1)S(1)} %pad_maximum_fusion), channel_id=1, source_target_pairs={{0,12},{4,8},{8,4},{12,0},{1,13},{5,9},{9,5},{13,1},{2,14},{6,10},... | collective-permute-start | bytes 1572872 | tf_op jit(solution)/shard_map/ppermute | solution.py:24
  45.4 1.3 %collective-permute-start.11 = (bf16[16,2,64,128]{3,2,1,0:T(8,128)(2,1)S(1)}, bf16[16,2,64,128]{3,2,1,0:T(8,128)(2,1)S(1)}, u32[]{:S(2)}, u32[]{:S(2)}) collective-permute-start(bf16[16,2,64,128]{3,2,1,0:T(8,128)(2,1)S(1)} %pad_maximum_fusion.2), channel_id=1, source_target_pairs={{0,48},{16,32},{32,16},{48,0},{1,49},{17,33},{33,17},{49,1},{2,50}... | collective-permute-start | bytes 1572872 | tf_op jit(solution)/shard_map/ppermute | solution.py:24
  47.8 3.4 %collective-permute-start.10 = (bf16[16,2,64,128]{3,2,1,0:T(8,128)(2,1)S(1)}, bf16[16,2,64,128]{3,2,1,0:T(8,128)(2,1)S(1)}, u32[]{:S(2)}, u32[]{:S(2)}) collective-permute-start(bf16[16,2,64,128]{3,2,1,0:T(8,128)(2,1)S(1)} %pad_maximum_fusion.1), channel_id=1, source_target_pairs={{0,4},{4,0},{8,12},{12,8},{1,5},{5,1},{9,13},{13,9},{2,6},{6,2},{1... | collective-permute-start | bytes 1572872 | tf_op jit(solution)/shard_map/ppermute | solution.py:24
  52.2 13.5 %attend.2 = (f32[29,8,128]{2,1,0:T(8,128)S(1)}, f32[29,8,128]{2,1,0:T(8,128)S(1)}, f32[29,128,128]{2,1,0:T(8,128)S(1)}, bf16[28,128,128]{2,1,0:T(8,128)(2,1)S(1)}) custom-call(s32[29,128]{1,0:T(8,128)S(1)} %pad.14.refs_0_, s32[29]{0:T(128)S(1)} %pad.15.refs_1_, bf16[28,64,128]{2,1,0:T(8,128)(2,1)S(1)} %bitcast.13, ...), custom_call_target="tpu_custom_call" | custom-call | flops 15032385536 | bytes 2097152 | tf_op jit(solution)/shard_map/attend/pallas_call | solution.py:189
  65.8 15.5 %attend.3 = (f32[29,64,128]{2,1,0:T(8,128)S(1)}, f32[29,64,128]{2,1,0:T(8,128)S(1)}) custom-call(s32[29,128]{1,0:T(8,128)S(1)} %pad.16.refs_0_, s32[29]{0:T(128)S(1)} %pad.17.refs_1_, bf16[28,128,128]{2,1,0:T(8,128)(2,1)S(1)} %get-tuple-element.23.refs_2_, bf16[16,2,64,128]{3,2,1,0:T(8,128)(2,1)S(1)} %collective-permute-done.9.refs_3_, ...), custom_call_target="tpu_custom_call" | custom-call | flops 15032385536 | bytes 2097152 | tf_op jit(solution)/shard_map/attend/pallas_call | solution.py:189
  82.2 2.5 %collective-permute-done.13.b_far = f32[29,64,128]{2,1,0:T(8,128)S(1)} collective-permute-done((f32[29,64,128]{2,1,0:T(8,128)S(1)}, f32[29,64,128]{2,1,0:T(8,128)S(1)}, u32[]{:S(2)}, u32[]{:S(2)}) %collective-permute-start.13) | collective-permute-done | bytes 950304 | tf_op jit(solution)/shard_map/ppermute | solution.py:24
  85.7 2.5 %merge.1 = bf16[28,64,128]{2,1,0:T(8,128)(2,1)} custom-call(f32[29,64,128]{2,1,0:T(8,128)} %copy-done.1, f32[29,64,128]{2,1,0:T(8,128)} %copy-done.4), custom_call_target="tpu_custom_call" | custom-call | tf_op jit(solution)/shard_map/merge/pallas_call | solution.py:248
  88.2 6.0 %all-to-all-start.2 = ((bf16[4,448,128]{2,1,0:T(8,128)(2,1)}), bf16[4,448,128]{2,1,0:T(8,128)(2,1)S(1)}, u32[]{:S(2)}, u32[]{:S(2)}) async-start(bf16[4,448,128]{2,1,0:T(8,128)(2,1)} %bitcast.14), calls=%async_computation.2 | async-start | bytes 917504 | tf_op jit(solution)/shard_map/all_to_all | solution.py:369
  94.8 15.0 %all-to-all-done.2 = bf16[4,448,128]{2,1,0:T(8,128)(2,1)S(1)} async-done(((bf16[4,448,128]{2,1,0:T(8,128)(2,1)}), bf16[4,448,128]{2,1,0:T(8,128)(2,1)S(1)}, u32[]{:S(2)}, u32[]{:S(2)}) %all-to-all-start.2) | async-done | bytes 458784 | tf_op jit(solution)/shard_map/all_to_all | solution.py:369
  110.7 1.9 %place.1 = bf16[64,3584]{1,0:T(8,128)(2,1)} custom-call(s32[28]{0:T(128)} %select_reduce_fusion.2.spot, bf16[28,64,128]{2,1,0:T(8,128)(2,1)} %bitcast.16), custom_call_target="tpu_custom_call" | custom-call | tf_op jit(solution)/shard_map/place/pallas_call | solution.py:269
  (57 shorter events, 11.2 us)
Async XLA Ops:
  0.0 10.3 %copy-start = (s32[128,28,128]{2,0,1:T(8,128)S(1)}, s32[128,28,128]{2,0,1:T(8,128)}, u32[]{:S(2)}) copy-start(s32[128,28,128]{2,0,1:T(8,128)} %param.9) | copy-start | bytes 5505028
  1.7 19.0 %all-to-all-start = ((bf16[8,2,64,128]{3,2,1,0:T(8,128)(2,1)}), bf16[8,2,64,128]{3,2,1,0:T(8,128)(2,1)S(1)}, u32[]{:S(2)}, u32[]{:S(2)}) async-start(bf16[8,2,64,128]{3,2,1,0:T(8,128)(2,1)} %split.2), calls=%async_computation | async-start | bytes 524288 | tf_op jit(solution)/shard_map/all_to_all | solution.py:346
  20.7 20.9 %all-to-all-start.1 = ((bf16[4,448,128]{2,1,0:T(8,128)(2,1)}), bf16[4,448,128]{2,1,0:T(8,128)(2,1)S(1)}, u32[]{:S(2)}, u32[]{:S(2)}) async-start(bf16[4,448,128]{2,1,0:T(8,128)(2,1)} %bitcast.15), calls=%async_computation.1 | async-start | bytes 917504 | tf_op jit(solution)/shard_map/all_to_all | solution.py:352
  24.2 5.1 %copy-start.3 = (bf16[4,2,64,128]{3,2,1,0:T(8,128)(2,1)}, bf16[4,2,64,128]{3,2,1,0:T(8,128)(2,1)S(1)}, u32[]{:S(2)}) copy-start(bf16[4,2,64,128]{3,2,1,0:T(8,128)(2,1)S(1)} %get-tuple-element.34) | copy-start | bytes 393220
  24.2 5.1 %collective-permute-start.1 = (bf16[4,2,64,128]{3,2,1,0:T(8,128)(2,1)S(1)}, bf16[4,2,64,128]{3,2,1,0:T(8,128)(2,1)S(1)}, u32[]{:S(2)}, u32[]{:S(2)}) collective-permute-start(bf16[4,2,64,128]{3,2,1,0:T(8,128)(2,1)S(1)} %get-tuple-element.34), channel_id=1, source_target_pairs={{0,16},{16,0},{32,48},{48,32},{1,17},{17,1},{33,49},{49,33},{2,18}... | collective-permute-start | bytes 393224 | tf_op jit(solution)/shard_map/ppermute | solution.py:24
  25.2 5.4 %collective-permute-start.5 = (bf16[4,2,64,128]{3,2,1,0:T(8,128)(2,1)S(1)}, bf16[4,2,64,128]{3,2,1,0:T(8,128)(2,1)S(1)}, u32[]{:S(2)}, u32[]{:S(2)}) collective-permute-start(bf16[4,2,64,128]{3,2,1,0:T(8,128)(2,1)S(1)} %get-tuple-element.33), channel_id=1, source_target_pairs={{0,4},{4,0},{8,12},{12,8},{1,5},{5,1},{9,13},{13,9},{2,6},{6,2},{1... | collective-permute-start | bytes 393224 | tf_op jit(solution)/shard_map/ppermute | solution.py:24
  30.0 7.7 %collective-permute-start.2 = (bf16[8,2,64,128]{3,2,1,0:T(8,128)(2,1)S(1)}, bf16[8,2,64,128]{3,2,1,0:T(8,128)(2,1)S(1)}, u32[]{:S(2)}, u32[]{:S(2)}) collective-permute-start(bf16[8,2,64,128]{3,2,1,0:T(8,128)(2,1)S(1)} %pad_maximum_fusion.4.refs_4_), channel_id=1, source_target_pairs={{0,48},{16,32},{32,16},{48,0},{1,49},{17,33},{33,17},{49,1},{2,50}... | collective-permute-start | bytes 786440 | tf_op jit(solution)/shard_map/ppermute | solution.py:24
  30.5 9.4 %copy-start.5 = (bf16[4,2,64,128]{3,2,1,0:T(8,128)(2,1)}, bf16[4,2,64,128]{3,2,1,0:T(8,128)(2,1)S(1)}, u32[]{:S(2)}) copy-start(bf16[4,2,64,128]{3,2,1,0:T(8,128)(2,1)S(1)} %collective-permute-done.5) | copy-start | bytes 393220
  30.6 9.3 %collective-permute-start.6 = (bf16[8,2,64,128]{3,2,1,0:T(8,128)(2,1)S(1)}, bf16[8,2,64,128]{3,2,1,0:T(8,128)(2,1)S(1)}, u32[]{:S(2)}, u32[]{:S(2)}) collective-permute-start(bf16[8,2,64,128]{3,2,1,0:T(8,128)(2,1)S(1)} %pad_maximum_fusion.5.refs_8_), channel_id=1, source_target_pairs={{0,12},{4,8},{8,4},{12,0},{1,13},{5,9},{9,5},{13,1},{2,14},{6,10},... | collective-permute-start | bytes 786440 | tf_op jit(solution)/shard_map/ppermute | solution.py:24
  32.7 8.9 %collective-permute-start.3 = (bf16[8,2,64,128]{3,2,1,0:T(8,128)(2,1)S(1)}, bf16[8,2,64,128]{3,2,1,0:T(8,128)(2,1)}, u32[]{:S(2)}, u32[]{:S(2)}) collective-permute-start(bf16[8,2,64,128]{3,2,1,0:T(8,128)(2,1)S(1)} %pad_maximum_fusion.4.refs_4_), channel_id=1, source_target_pairs={{0,4},{4,0},{8,12},{12,8},{1,5},{5,1},{9,13},{13,9},{2,6},{6,2},{1... | collective-permute-start | bytes 786440 | tf_op jit(solution)/shard_map/ppermute | solution.py:24
  34.7 9.7 %collective-permute-start.7 = (bf16[8,2,64,128]{3,2,1,0:T(8,128)(2,1)S(1)}, bf16[8,2,64,128]{3,2,1,0:T(8,128)(2,1)}, u32[]{:S(2)}, u32[]{:S(2)}) collective-permute-start(bf16[8,2,64,128]{3,2,1,0:T(8,128)(2,1)S(1)} %pad_maximum_fusion.5.refs_8_), channel_id=1, source_target_pairs={{0,16},{16,0},{32,48},{48,32},{1,17},{17,1},{33,49},{49,33},{2,18}... | collective-permute-start | bytes 786440 | tf_op jit(solution)/shard_map/ppermute | solution.py:24
  37.6 9.1 %collective-permute-start.4 = (bf16[8,2,64,128]{3,2,1,0:T(8,128)(2,1)S(1)}, bf16[8,2,64,128]{3,2,1,0:T(8,128)(2,1)}, u32[]{:S(2)}, u32[]{:S(2)}) collective-permute-start(bf16[8,2,64,128]{3,2,1,0:T(8,128)(2,1)S(1)} %collective-permute-done.2.refs_5_), channel_id=1, source_target_pairs={{0,12},{4,8},{8,4},{12,0},{1,13},{5,9},{9,5},{13,1},{2,14},{6,10},... | collective-permute-start | bytes 786440 | tf_op jit(solution)/shard_map/ppermute | solution.py:24
  39.9 11.2 %collective-permute-start.8 = (bf16[8,2,64,128]{3,2,1,0:T(8,128)(2,1)S(1)}, bf16[8,2,64,128]{3,2,1,0:T(8,128)(2,1)}, u32[]{:S(2)}, u32[]{:S(2)}) collective-permute-start(bf16[8,2,64,128]{3,2,1,0:T(8,128)(2,1)S(1)} %collective-permute-done.6.refs_9_), channel_id=1, source_target_pairs={{0,48},{16,32},{32,16},{48,0},{1,49},{17,33},{33,17},{49,1},{2,50}... | collective-permute-start | bytes 786440 | tf_op jit(solution)/shard_map/ppermute | solution.py:24
  41.6 10.6 %collective-permute-start = (bf16[28,64,128]{2,1,0:T(8,128)(2,1)S(1)}, bf16[28,64,128]{2,1,0:T(8,128)(2,1)S(1)}, u32[]{:S(2)}, u32[]{:S(2)}) collective-permute-start(bf16[28,64,128]{2,1,0:T(8,128)(2,1)S(1)} %bitcast.12), channel_id=1, source_target_pairs={{0,1},{1,0},{2,3},{3,2},{4,5},{5,4},{6,7},{7,6},{8,9},{9,8},{10,11... | collective-permute-start | bytes 1376264 | tf_op jit(solution)/shard_map/ppermute | solution.py:24
  42.7 23.0 %collective-permute-start.9 = (bf16[16,2,64,128]{3,2,1,0:T(8,128)(2,1)S(1)}, bf16[16,2,64,128]{3,2,1,0:T(8,128)(2,1)S(1)}, u32[]{:S(2)}, u32[]{:S(2)}) collective-permute-start(bf16[16,2,64,128]{3,2,1,0:T(8,128)(2,1)S(1)} %pad_maximum_fusion), channel_id=1, source_target_pairs={{0,12},{4,8},{8,4},{12,0},{1,13},{5,9},{9,5},{13,1},{2,14},{6,10},... | collective-permute-start | bytes 1572872 | tf_op jit(solution)/shard_map/ppermute | solution.py:24
  45.4 20.3 %collective-permute-start.11 = (bf16[16,2,64,128]{3,2,1,0:T(8,128)(2,1)S(1)}, bf16[16,2,64,128]{3,2,1,0:T(8,128)(2,1)S(1)}, u32[]{:S(2)}, u32[]{:S(2)}) collective-permute-start(bf16[16,2,64,128]{3,2,1,0:T(8,128)(2,1)S(1)} %pad_maximum_fusion.2), channel_id=1, source_target_pairs={{0,48},{16,32},{32,16},{48,0},{1,49},{17,33},{33,17},{49,1},{2,50}... | collective-permute-start | bytes 1572872 | tf_op jit(solution)/shard_map/ppermute | solution.py:24
  47.8 18.0 %collective-permute-start.10 = (bf16[16,2,64,128]{3,2,1,0:T(8,128)(2,1)S(1)}, bf16[16,2,64,128]{3,2,1,0:T(8,128)(2,1)S(1)}, u32[]{:S(2)}, u32[]{:S(2)}) collective-permute-start(bf16[16,2,64,128]{3,2,1,0:T(8,128)(2,1)S(1)} %pad_maximum_fusion.1), channel_id=1, source_target_pairs={{0,4},{4,0},{8,12},{12,8},{1,5},{5,1},{9,13},{13,9},{2,6},{6,2},{1... | collective-permute-start | bytes 1572872 | tf_op jit(solution)/shard_map/ppermute | solution.py:24
  52.1 13.6 %collective-permute-start.12 = (bf16[16,2,64,128]{3,2,1,0:T(8,128)(2,1)S(1)}, bf16[16,2,64,128]{3,2,1,0:T(8,128)(2,1)S(1)}, u32[]{:S(2)}, u32[]{:S(2)}) collective-permute-start(bf16[16,2,64,128]{3,2,1,0:T(8,128)(2,1)S(1)} %pad_maximum_fusion.3), channel_id=1, source_target_pairs={{0,16},{16,0},{32,48},{48,32},{1,17},{17,1},{33,49},{49,33},{2,18}... | collective-permute-start | bytes 1572872 | tf_op jit(solution)/shard_map/ppermute | solution.py:24
  81.3 0.9 copy-start.1
  82.2 12.0 %copy-start.7 = (s32[28]{0:T(128)S(1)}, s32[28]{0:T(128)}, u32[]{:S(2)}) copy-start(s32[28]{0:T(128)} %param.11) | copy-start | bytes 340
  82.2 2.5 %collective-permute-start.13 = (f32[29,64,128]{2,1,0:T(8,128)S(1)}, f32[29,64,128]{2,1,0:T(8,128)S(1)}, u32[]{:S(2)}, u32[]{:S(2)}) collective-permute-start(f32[29,64,128]{2,1,0:T(8,128)S(1)} %get-tuple-element.28), channel_id=1, source_target_pairs={{0,1},{1,0},{2,3},{3,2},{4,5},{5,4},{6,7},{7,6},{8,9},{9,8},{10,11... | collective-permute-start | bytes 2850824 | tf_op jit(solution)/shard_map/ppermute | solution.py:24
  84.7 1.0 copy-start.4
  88.2 21.7 %all-to-all-start.2 = ((bf16[4,448,128]{2,1,0:T(8,128)(2,1)}), bf16[4,448,128]{2,1,0:T(8,128)(2,1)S(1)}, u32[]{:S(2)}, u32[]{:S(2)}) async-start(bf16[4,448,128]{2,1,0:T(8,128)(2,1)} %bitcast.14), calls=%async_computation.2 | async-start | bytes 917504 | tf_op jit(solution)/shard_map/all_to_all | solution.py:369
  109.9 0.8 copy-start.2
  (1 other events, 0.7 us)
